TPU v7x, 32 devices: a whole 2x2x4 slice. The times are simulated.
32 devices in a mesh: dp: 2 (over y), fsdp: 8 (over z, core), tensor: 2 (over x).
Axes of the slice: x: 2, y: 2, z: 4, core: 2. Of those that a mesh axis runs over, the one named last changes fastest.
Arguments:
- attn_out: bfloat16 [2048, 2560], P(('dp', 'fsdp')), may hold values from -6 to 6
- cotangent: bfloat16 [2048, 5120], P(('dp', 'fsdp'), 'tensor'), may hold values from -6 to 6
- old_weights: bfloat16 [3, 2048, 4096], P(None, 'tensor', 'fsdp'), may hold values from -0.125 to 0.125
- depth_coef: float32 [2], replicated, may hold values from 0.3 to 1
- depth_pick: int32 [2], replicated, may hold values from 0 to 2
- in_blocks: bfloat16 [20, 2, 128, 128], replicated, may hold values from -0.3125 to 0.3125
- in_cols: int32 [20, 2], replicated, may hold values from 0 to 15, all different within a row
- out_blocks: bfloat16 [40, 2, 128, 128], P('tensor'), may hold values from -0.375 to 0.375
- out_cols: int32 [40, 2], P('tensor'), may hold values from 0 to 31, all different within a row
Outputs:
- grown_out: bfloat16 [2048, 5120], P(('dp', 'fsdp'), 'tensor')
- grad_attn: bfloat16 [2048, 2560], P(('dp', 'fsdp'), 'tensor')
- grad_in_blocks: float32 [20, 2, 128, 128], P('tensor')
- grad_out_blocks: float32 [40, 2, 128, 128], P('tensor')
Inputs may be any that keep to these rules, and one draw needn't show every extreme that they name: `in_cols`: each row names 2 different old head blocks; every old head block is named by some row. `out_cols`: each row names 2 different old width blocks; every old width block is named by some row.
All inputs are finite; a program needn't handle non-finite values.
Results may differ from a plain program's by a relative error of at most 0.0095.
Values may be sent and summed in bfloat16 or wider, within the bound.
A program may use at most 64 MiB of HBM per device.

v0:
```python
import jax
import jax.numpy as jnp
from jax import lax
from jax.sharding import PartitionSpec as P

HEAD = 128
D_OLD = 4096
HG_OLD = 16
HG_NEW = 20
DEPTH_K = 2
BO_OLD = 32


def gathered_mix(mixed_weight):
    return lax.all_gather(mixed_weight, "fsdp", axis=1, tiled=True)


def local(
    attn_out,
    cotangent,
    old_weights,
    depth_coef,
    depth_pick,
    in_blocks,
    in_cols,
    out_blocks,
    out_cols,
):
    highest = lax.Precision.HIGHEST
    tok_rows = attn_out.shape[0]
    tensor_half = lax.axis_index("tensor")
    tensor_count = lax.axis_size("tensor")
    local_old = old_weights.shape[1]
    local_blocks = local_old // HEAD
    rows_in = HG_NEW // tensor_count
    mixed_weight = jnp.zeros(old_weights.shape[1:], jnp.float32)
    for layer_slot in range(DEPTH_K):
        picked = lax.dynamic_index_in_dim(old_weights, depth_pick[layer_slot], 0, keepdims=False)
        mixed_weight = mixed_weight + depth_coef[layer_slot] * picked.astype(jnp.float32)
    mixed_weight = mixed_weight.astype(jnp.bfloat16)
    attn_blocks = attn_out.reshape(tok_rows, HG_NEW, HEAD)
    products = jnp.einsum(
        "trd,rkde->trke", attn_blocks, in_blocks, preferred_element_type=jnp.float32
    )
    local_cols = tensor_half * local_blocks + jnp.arange(local_blocks, dtype=jnp.int32)
    in_hot = (in_cols[:, :, None] == local_cols[None, None, :]).astype(jnp.float32)
    hidden_local = jnp.einsum("trke,rkc->tce", products, in_hot, precision=highest)
    hidden_local = hidden_local.reshape(tok_rows, local_old).astype(jnp.bfloat16)
    full_mix = gathered_mix(mixed_weight)
    old_part = jnp.dot(hidden_local, full_mix, preferred_element_type=jnp.float32)
    old_out = lax.psum(old_part.astype(jnp.bfloat16), "tensor")
    old_selected = jnp.take(old_out.reshape(tok_rows, BO_OLD, HEAD), out_cols, axis=1)
    grown_out = jnp.einsum(
        "trkd,rkde->tre", old_selected, out_blocks, preferred_element_type=jnp.float32
    )
    grown_out = grown_out.reshape(tok_rows, -1).astype(jnp.bfloat16)
    cot_blocks = cotangent.reshape(tok_rows, out_blocks.shape[0], HEAD)
    backward_terms = jnp.einsum(
        "tre,rkde->trkd", cot_blocks, out_blocks, preferred_element_type=jnp.float32
    )
    out_hot = (out_cols[:, :, None] == jnp.arange(BO_OLD, dtype=jnp.int32)[None, None, :]).astype(
        jnp.float32
    )
    grad_part = jnp.einsum("trkd,rkc->tcd", backward_terms, out_hot, precision=highest).reshape(
        tok_rows, D_OLD
    )
    old_grad = lax.psum(grad_part.astype(jnp.bfloat16), "tensor")
    hidden_grad_local = jnp.einsum(
        "to,fo->tf", old_grad, full_mix, preferred_element_type=jnp.float32
    ).astype(jnp.bfloat16)
    hidden_grad = lax.all_gather(hidden_grad_local, "tensor", axis=1, tiled=True)
    my_in_blocks = lax.dynamic_slice_in_dim(in_blocks, tensor_half * rows_in, rows_in, 0)
    my_in_cols = lax.dynamic_slice_in_dim(in_cols, tensor_half * rows_in, rows_in, 0)
    grad_selected = jnp.take(hidden_grad.reshape(tok_rows, HG_OLD, HEAD), my_in_cols, axis=1)
    grad_attn = jnp.einsum(
        "trke,rkde->trd", grad_selected, my_in_blocks, preferred_element_type=jnp.float32
    )
    grad_attn = grad_attn.reshape(tok_rows, rows_in * HEAD).astype(jnp.bfloat16)
    my_attn = lax.dynamic_slice_in_dim(attn_blocks, tensor_half * rows_in, rows_in, 1)
    in_terms = jnp.einsum(
        "trd,trke->rkde", my_attn, grad_selected, preferred_element_type=jnp.float32
    )
    out_terms = jnp.einsum(
        "trkd,tre->rkde", old_selected, cot_blocks, preferred_element_type=jnp.float32
    )
    in_sum, out_sum = lax.psum((in_terms, out_terms), ("dp", "fsdp"))
    grad_scale = float(tok_rows * lax.axis_size("dp") * lax.axis_size("fsdp")) ** (-0.5)
    return (grown_out, grad_attn, in_sum * grad_scale, out_sum * grad_scale)


def solution(mesh):
    placed = (
        P(("dp", "fsdp"), None),
        P(("dp", "fsdp"), "tensor"),
        P(None, "tensor", "fsdp"),
        P(),
        P(),
        P(),
        P(),
        P("tensor", None, None, None),
        P("tensor", None),
    )
    return jax.shard_map(
        local,
        mesh=mesh,
        in_specs=placed,
        out_specs=(
            P(("dp", "fsdp"), "tensor"),
            P(("dp", "fsdp"), "tensor"),
            P("tensor", None, None, None),
            P("tensor", None, None, None),
        ),
        check_vma=False,
    )
```

profile of v0, /device:TPU:9, one launch (start us, length us, event | category | flops | bytes accessed | tf_op | source)
XLA Modules:
  0.0 314.8 jit_solution(11088488509105804885)
XLA Ops:
  7.2 0.0 copy-start
  7.2 0.0 all-gather.3.cloned.1.call-start
  7.2 1.3 fusion.55
  11.2 1.3 fusion.54
  13.8 0.0 copy-start.6
  13.8 4.2 %add_convert_fusion = bf16[1,1024,512]{2,1,0:T(8,128)(2,1)} fusion(bf16[3,1024,512]{2,1,0:T(8,128)(2,1)} %param.11, s32[]{:T(128)S(6)} %select_n.32, f32[]{:T(128)} %bitcast.10, s32[]{:T(128)S(6)} %select_n.31, f32[]{:T(128)} %bitcast.8), kind=kLoop, calls=%fused_computation.12 | loop fusion | flops 3145728 | bytes 3145744 | tf_op jit(solution)/shard_map/convert_element_type | solution.py:40
  18.0 0.0 all-gather.3.cloned.1.call-update
  18.0 0.0 all-reduce.7.cloned.1.call-start
  18.1 1.4 copy.27
  19.5 0.0 copy-start.1
  19.5 0.0 copy-done.6
  19.5 2.0 fusion.56
  21.6 0.0 copy-done.1
  21.6 0.0 copy-start.7
  21.6 3.6 %copy.45 = f32[20,2,128,128]{2,0,1,3:T(8,128)} copy(f32[20,2,128,128]{3,2,1,0:T(8,128)} %fusion.56) | data formatting | bytes 5242880 | tf_op jit(solution)/shard_map/trd,rkde->trke/dot_general | solution.py:42
  25.2 0.0 copy-done.7
  25.2 0.3 copy.34
  25.5 0.0 copy-done
  25.5 2.0 fusion.57
  27.5 0.0 copy-start.9
  27.5 3.7 %copy.51 = f32[20,2,128,128]{2,0,1,3:T(8,128)} copy(f32[20,2,128,128]{3,2,1,0:T(8,128)} %fusion.57) | data formatting | bytes 5242880 | tf_op jit(solution)/shard_map/tre,rkde->trkd/dot_general | solution.py:58
  31.2 0.0 copy-done.9
  31.2 3.3 %bitcast_convert_fusion = bf16[32,128,128]{2,0,1:T(8,128)(2,1)S(1)} fusion(f32[20,2,128,128]{2,0,1,3:T(8,128)} %copy.51, s32[20,2]{0,1:T(2,128)S(1)} %copy-done.9), kind=kOutput, calls=%fused_computation.11 | convolution fusion | flops 252183808 | bytes 3670176 | tf_op jit(solution)/shard_map/trkd,rkc->tcd/dot_general | solution.py:64
  34.5 0.0 copy-start.8
  34.6 1.4 copy.71
  36.0 0.0 copy-done.8
  36.0 3.1 fusion.24
  39.0 60.1 %all-gather.3.cloned.1.call-done = bf16[1,1024,4096]{2,1,0:T(8,128)(2,1)} async-done(((bf16[1,1024,512]{2,1,0:T(8,128)(2,1)}), bf16[1,1024,4096]{2,1,0:T(8,128)(2,1)}) %all-gather.3.cloned.1.call-update) | async-done | bytes 8388624 | tf_op jit(solution)/shard_map/all_gather | solution.py:15
  99.1 4.7 %fusion.13 = bf16[16,32,8,128]{3,2,1,0:T(8,128)(2,1)S(1)} fusion(bf16[1,1024,4096]{2,1,0:T(8,128)(2,1)} %all-gather.3.cloned.1.call-done, bf16[16,8,8,128]{3,2,1,0:T(8,128)(2,1)S(1)} %bitcast.126), kind=kOutput, calls=%fused_computation.15 | convolution fusion | flops 1074266112 | bytes 9699328 | tf_op jit(solution)/shard_map/dot_general | solution.py:50
  103.8 1.3 copy.72
  105.1 0.0 all-reduce.7.cloned.1.call-update
  105.1 0.0 all-reduce.5.cloned.1.call-start
  105.1 0.1 compare_and_fusion
  105.2 0.1 copy.35
  105.3 0.1 reshape.66
  105.4 0.1 copy.33
  105.5 0.1 copy.29
  105.6 0.1 reshape.58
  105.7 0.1 copy.26
  105.9 63.3 %all-reduce.7.cloned.1.call-done = (bf16[128,32,128]{2,0,1:T(8,128)(2,1)}, bf16[128,4096]{1,0:T(8,128)(2,1)}) async-done(((bf16[128,32,128]{2,0,1:T(8,128)(2,1)}, bf16[128,4096]{1,0:T(8,128)(2,1)}), (bf16[128,32,128]{2,0,1:T(8,128)(2,1)}, bf16[128,4096]{1,0:T(8,128)(2,1)})) %all-reduce.7.cloned.1.call-update) | async-done | bytes 2097168 | tf_op jit(solution)/shard_map/psum | solution.py:51
  169.2 6.6 %fusion.27 = bf16[128,1024]{1,0:T(8,128)(2,1)S(1)} fusion(bf16[128,4096]{1,0:T(8,128)(2,1)} %get-tuple-element.15, bf16[1,1024,4096]{2,1,0:T(8,128)(2,1)} %all-gather.3.cloned.1.call-done), kind=kOutput, calls=%fused_computation.26 | convolution fusion | flops 1073872896 | bytes 9699328 | tf_op jit(solution)/shard_map/to,fo->tf/dot_general | solution.py:68
  175.8 8.0 %all_gather.7 = bf16[128,2048]{1,0:T(8,128)(2,1)S(1)} all-gather(bf16[128,1024]{1,0:T(8,128)(2,1)S(1)} %fusion.27), channel_id=1, replica_groups=mesh['dp'=2,'fsdp'=8,'tensor'=2] {'tensor'}, dimensions={1}, use_global_device_ids=true | all-gather | bytes 786432 | tf_op jit(solution)/shard_map/all_gather | solution.py:71
  183.8 0.1 copy_bitcast_fusion.2
  184.0 0.7 gather_fusion.1
  184.6 1.1 copy.37
  185.7 3.1 gather_fusion
  188.8 1.8 copy.30
  190.6 0.0 copy-start.2
  190.6 0.0 copy-start.3
  190.6 2.0 fusion.17
  192.6 0.0 copy-done.2
  192.6 0.0 copy-done.3
  192.6 1.4 convolution_bitcast_fusion
  194.1 0.0 all-reduce.5.cloned.1.call-update
  194.1 1.1 copy-done.4
  195.2 2.2 fusion.23
  197.4 1.9 copy.42
  199.2 0.6 fusion.16
  199.9 1.1 copy.41
  200.9 102.0 %all-reduce.5.cloned.1.call-done = (f32[10,2,128,128]{2,3,1,0:T(8,128)}, f32[20,2,128,128]{3,2,1,0:T(8,128)}) async-done(((f32[10,2,128,128]{2,3,1,0:T(8,128)}, f32[20,2,128,128]{3,2,1,0:T(8,128)}), (f32[10,2,128,128]{2,3,1,0:T(8,128)}, f32[20,2,128,128]{3,2,1,0:T(8,128)})) %all-reduce.5.cloned.1.call-update) | async-done | bytes 3932176 | tf_op jit(solution)/shard_map/psum | solution.py:86
  302.9 3.7 %broadcast_multiply_fusion = f32[20,2,128,128]{3,2,1,0:T(8,128)} fusion(f32[20,2,128,128]{3,2,1,0:T(8,128)} %get-tuple-element.13), kind=kLoop, calls=%fused_computation.20 | loop fusion | flops 655360 | bytes 5242880 | tf_op jit(solution)/shard_map/mul | solution.py:88
  306.7 0.0 copy-done.5
  306.7 0.1 broadcast_multiply_fusion.1
  306.8 1.5 copy.43
  (7 shorter events, 0.0 us)
Async XLA Ops:
  7.2 18.4 %copy-start = (bf16[20,2,128,128]{3,2,1,0:T(8,128)(2,1)S(1)}, bf16[20,2,128,128]{3,2,1,0:T(8,128)(2,1)}, u32[]{:S(2)}) copy-start(bf16[20,2,128,128]{3,2,1,0:T(8,128)(2,1)} %param.16) | copy-start | bytes 3932164
  7.2 91.9 %all-gather.3.cloned.1.call-start = ((), (), s32[]{:S(2)}) async-start(), calls=%async_computation | async-start | bytes 9437184 | tf_op jit(solution)/shard_map/all_gather | solution.py:15
  13.8 5.7 %copy-start.6 = (bf16[20,2,128,128]{3,2,1,0:T(8,128)(2,1)S(1)}, bf16[20,2,128,128]{3,2,1,0:T(8,128)(2,1)}, u32[]{:S(2)}) copy-start(bf16[20,2,128,128]{3,2,1,0:T(8,128)(2,1)} %param.14) | copy-start | bytes 3932164
  18.0 151.1 %all-reduce.7.cloned.1.call-start = ((), (), s32[]{:S(2)}) async-start(), calls=%async_computation.2 | async-start | bytes 4194304 | tf_op jit(solution)/shard_map/psum | solution.py:51
  19.5 2.1 copy-start.1
  21.6 3.6 %copy-start.7 = (bf16[128,2560]{1,0:T(8,128)(2,1)S(1)}, bf16[128,2560]{1,0:T(8,128)(2,1)}, u32[]{:S(2)}) copy-start(bf16[128,2560]{1,0:T(8,128)(2,1)} %param.10) | copy-start | bytes 1966084
  27.5 3.7 %copy-start.9 = (s32[20,2]{0,1:T(2,128)S(1)}, s32[20,2]{0,1:T(2,128)}, u32[]{:S(2)}) copy-start(s32[20,2]{0,1:T(2,128)} %param.17) | copy-start | bytes 484
  34.5 1.4 copy-start.8
  105.1 197.9 %all-reduce.5.cloned.1.call-start = ((), (), s32[]{:S(2)}) async-start(), calls=%async_computation.1 | async-start | bytes 7864320 | tf_op jit(solution)/shard_map/psum | solution.py:86
  190.6 2.1 copy-start.2
  190.6 2.1 copy-start.3
  194.1 1.1 copy-start.4
  302.9 3.7 %copy-start.5 = (f32[10,2,128,128]{2,3,1,0:T(8,128)S(1)}, f32[10,2,128,128]{2,3,1,0:T(8,128)}, u32[]{:S(2)}) copy-start(f32[10,2,128,128]{2,3,1,0:T(8,128)} %get-tuple-element.12) | copy-start | bytes 3932164
Sparse Core Ops, SparseCore 0:
  18.1 80.9 all-gather.2
  105.2 63.9 all-reduce.6
  194.2 108.6 all-reduce.4
where the time goes:
time: 318 us; the launch traced here: 315 us
  waiting for transfers between devices  225 us (71%)
  matrix products  28 us (9%)
  local copies, waits for them, and re-layouts  27.2 us (9%)
  between operations  17.8 us (6%)
  other arithmetic  8.15 us (3%)
  blocking collectives  8.03 us (3%)
    psum x1, waiting for transfers between devices, local(): in_sum, out_sum = lax.psum((in_terms, out_terms), ('dp', 'fsdp'))  102 us
    psum x1, waiting for transfers between devices, local(): old_out = lax.psum(old_part.astype(jnp.bfloat16), 'tensor')  63.3 us
    all_gather x1, waiting for transfers between devices, gathered_mix(): return lax.all_gather(mixed_weight, 'fsdp', axis=1, tiled=True)  60.1 us
    unnamed x26, local copies, waits for them, and re-layouts  8.67 us
    all_gather x1, blocking collectives, local(): lax.all_gather(hidden_grad_local, 'tensor', axis=1, tiled=True)  8.03 us
    dot_general x1, matrix products, local(): jnp.einsum('to,fo->tf', old_grad, full_mix, preferred_element_type=jnp.fl...  6.62 us
  transfers between devices with their start and end apart: 3, of which 3 were waited for; matrix products, arithmetic and copies ran while one was open for 9% of the time, Pallas kernels for 0%

commit v1 on v0

v1 whole, which is shorter than its diff:
```python
import functools

import jax
import jax.numpy as jnp
from jax import lax
from jax.experimental import pallas as pl
from jax.experimental.pallas import tpu as pltpu
from jax.sharding import PartitionSpec as P

HEAD = 128
MESH = pl.DeviceIdType.MESH
F32 = jnp.float32
BF16 = jnp.bfloat16


def dot(a, b, ca=1, cb=0):
    return lax.dot_general(a, b, (((ca,), (cb,)), ((), ())), preferred_element_type=F32)


def kernel(
    dims,
    pick,
    coef,
    in_cols,
    out_cols,
    in_ptr,
    out_ptr,
    attn,
    cot,
    old_w,
    in_b,
    out_b,
    grown,
    gattn,
    terms,
    w_all,
    sums,
    og_mine,
    og_theirs,
    p_mine,
    p_theirs,
    oo,
    hid,
    hg_acc,
    hg_all,
    w_send,
    w_recv,
    og_send,
    og_recv,
    p_send,
    p_recv,
    hg_send,
    hg_recv,
):
    zs, depth_k, k_in, k_out = dims
    shard = w_all.shape[2]
    feats = w_all.shape[1]
    half_rows = feats // 2
    nb = shard // HEAD
    nl = feats // HEAD
    n_out = og_mine.shape[0]
    pairs_in = in_cols.shape[0]
    pairs_out = out_cols.shape[0]
    rows_all = pairs_in // k_in
    rows_out = pairs_out // k_out
    rows_in = gattn.shape[1] // HEAD

    dp = lax.axis_index("dp")
    fs = lax.axis_index("fsdp")
    tn = lax.axis_index("tensor")
    z = fs // 2
    core = fs % 2
    h = dp % 2
    o = 1 - h
    other_core = {"fsdp": 2 * z + 1 - core}
    other_dp = {"dp": dp + 1 - 2 * h}
    other_tn = {"tensor": 1 - tn}
    above = {"fsdp": fs + 2}
    below = {"fsdp": fs - 2}

    def rows_of(half):
        return pl.ds(pl.multiple_of(half * half_rows, half_rows), half_rows)

    def w_copy(f, half, kind, to):
        piece = w_all.at[f, rows_of(half)]
        return pltpu.make_async_remote_copy(
            src_ref=piece,
            dst_ref=piece,
            send_sem=w_send.at[f, half, kind],
            recv_sem=w_recv.at[f, half],
            device_id=to,
            device_id_type=MESH,
        )

    def chunk_copy(src, dst, send, recv, f):
        part = pl.ds(f * nb, nb)
        return pltpu.make_async_remote_copy(
            src_ref=src.at[part],
            dst_ref=dst.at[part],
            send_sem=send.at[f],
            recv_sem=recv.at[f],
            device_id=other_tn,
            device_id_type=MESH,
        )

    def hg_copy(half):
        part = hg_all.at[pl.ds(half * nl, nl)]
        return pltpu.make_async_remote_copy(
            src_ref=part,
            dst_ref=part,
            send_sem=hg_send,
            recv_sem=hg_recv,
            device_id=other_tn,
            device_id_type=MESH,
        )

    barrier = pltpu.get_barrier_semaphore()
    for to in (other_core, other_dp, other_tn):
        pl.semaphore_signal(barrier, inc=1, device_id=to, device_id_type=MESH)

    @pl.when(z > 0)
    def _():
        pl.semaphore_signal(barrier, inc=1, device_id=below, device_id_type=MESH)

    @pl.when(z < zs - 1)
    def _():
        pl.semaphore_signal(barrier, inc=1, device_id=above, device_id_type=MESH)

    inner = (z > 0).astype(jnp.int32) + (z < zs - 1).astype(jnp.int32)
    pl.semaphore_wait(barrier, 3 + inner)

    mix_rows = 64

    def mix(half):
        def body(i, _):
            part = pl.ds(pl.multiple_of(half * half_rows + i * mix_rows, mix_rows), mix_rows)
            total = coef[0] * old_w[pick[0], part, :].astype(F32)
            for j in range(1, depth_k):
                total = total + coef[j] * old_w[pick[j], part, :].astype(F32)
            w_all[fs, part, :] = total.astype(BF16)
            return 0

        lax.fori_loop(0, half_rows // mix_rows, body, 0)

    mix(h)

    @pl.when(z < zs - 1)
    def _():
        w_copy(fs, h, 0, above).start()

    @pl.when(z > 0)
    def _():
        w_copy(fs, h, 1, below).start()

    w_copy(fs, h, 3, other_core).start()
    mix(o)
    w_copy(fs, o, 3, other_core).start()

    sums[pairs_out] = jnp.zeros((HEAD, HEAD), F32)

    def back_row(r, _):
        cols = pl.ds(pl.multiple_of(r * HEAD, HEAD), HEAD)
        for k in range(k_out):
            j = r * k_out + k
            sums[j] = dot(cot[:, cols], out_b[j], 1, 1) + sums[out_ptr[j]]
        return 0

    lax.fori_loop(0, rows_out, back_row, 0, unroll=4)

    def back_block(b, _):
        og_mine[b] = sums[out_ptr[pairs_out + b]].astype(BF16)
        return 0

    lax.fori_loop(0, n_out, back_block, 0, unroll=4)

    def over_shards(s, body):
        def one(i, _):
            zz = z - s + 2 * s * (i // 2)
            cc = (core + i) % 2
            live = (zz >= 0) & (zz < zs) & ((s > 0) | (i < 2))

            @pl.when(live)
            def _():
                body(zz * 2 + cc, i % 2)

            return 0

        lax.fori_loop(0, 4, one, 0)

    def og_start(s, _):
        over_shards(s, lambda f, mine: chunk_copy(og_mine, og_theirs, og_send, og_recv, f).start())
        return 0

    lax.fori_loop(0, zs, og_start, 0)

    sums[pairs_in] = jnp.zeros((HEAD, HEAD), F32)

    def hid_row(r, _):
        cols = pl.ds(pl.multiple_of(r * HEAD, HEAD), HEAD)
        for k in range(k_in):
            j = r * k_in + k
            sums[j] = dot(attn[:, cols], in_b[j]) + sums[in_ptr[j]]
        return 0

    lax.fori_loop(0, rows_all, hid_row, 0, unroll=4)
    for b in range(nl):
        hid[:, b * HEAD : (b + 1) * HEAD] = sums[in_ptr[pairs_in + tn * nl + b]].astype(BF16)

    hg_acc[...] = jnp.zeros_like(hg_acc)

    def forward(f, s):
        part = dot(hid[...], w_all[f]).astype(BF16)
        for b in range(nb):
            p_mine[f * nb + b] = part[:, b * HEAD : (b + 1) * HEAD]
        chunk_copy(p_mine, p_theirs, p_send, p_recv, f).start()

    def backward(f, flip):
        chunk_copy(og_mine, og_theirs, og_send, og_recv, f).wait_recv()
        blocks = [
            (og_mine[f * nb + b].astype(F32) + og_theirs[f * nb + b].astype(F32)).astype(BF16)
            for b in range(nb)
        ]
        hg_acc[...] += dot(jnp.concatenate(blocks, axis=1), w_all[f], 1, 1)

    def step(s, _):
        for way in range(2):
            zz = z - s + 2 * s * way
            nxt = z + 1 - 2 * way
            f = 2 * zz + core

            @pl.when((zz >= 0) & (zz < zs))
            def _():
                w_copy(f, h, way, other_dp).wait_recv()

                @pl.when((nxt >= 0) & (nxt < zs))
                def _():
                    w_copy(f, h, way, above if way == 0 else below).start()

                w_copy(f, h, 2, other_dp).start()
                w_copy(f, h, 3, other_core).start()

        def first(f, flip):
            @pl.when(flip == 1)
            def _():
                w_copy(f, 0, 3, other_core).wait_recv()
                w_copy(f, 1, 3, other_core).wait_recv()

            forward(f, s)

        over_shards(s - 1, first)

        for way in range(2):
            zz = z - s + 2 * s * way
            f = 2 * zz + core

            @pl.when((zz >= 0) & (zz < zs))
            def _():
                w_copy(f, o, 2, other_dp).wait_recv()
                w_copy(f, o, 3, other_core).start()

        @pl.when(s >= 2)
        def _():
            over_shards(s - 2, backward)

        return 0

    lax.fori_loop(1, zs + 2, step, 0)

    for b in range(nl):
        hg_all[tn * nl + b] = hg_acc[:, b * HEAD : (b + 1) * HEAD].astype(BF16)
    hg_copy(tn).start()

    def add_shard(f, _):
        chunk_copy(p_mine, p_theirs, p_send, p_recv, f).wait_recv()
        for b in range(nb):
            oo[f * nb + b] = (
                p_mine[f * nb + b].astype(F32) + p_theirs[f * nb + b].astype(F32)
            ).astype(BF16)
        return 0

    lax.fori_loop(0, 2 * zs, add_shard, 0)

    def out_row(r, _):
        cols = pl.ds(pl.multiple_of(r * HEAD, HEAD), HEAD)
        total = None
        for k in range(k_out):
            j = r * k_out + k
            block = oo[out_cols[j]]
            term = dot(block, out_b[j])
            total = term if total is None else total + term
            terms[j] = dot(block, cot[:, cols], 0, 0).astype(BF16)
        grown[:, cols] = total.astype(BF16)
        return 0

    lax.fori_loop(0, rows_out, out_row, 0, unroll=4)

    hg_copy(1 - tn).wait_recv()

    def in_row(r, _):
        cols = pl.ds(pl.multiple_of(r * HEAD, HEAD), HEAD)
        mine = tn * rows_in + r
        mine_cols = pl.ds(pl.multiple_of(mine * HEAD, HEAD), HEAD)
        total = None
        for k in range(k_in):
            j = mine * k_in + k
            block = hg_all[in_cols[j]]
            term = dot(block, in_b[j], 1, 1)
            total = term if total is None else total + term
            terms[pairs_out + r * k_in + k] = dot(attn[:, mine_cols], block, 0, 0).astype(BF16)
        gattn[:, cols] = total.astype(BF16)
        return 0

    lax.fori_loop(0, rows_in, in_row, 0, unroll=2)

    def send_done(f, _):
        chunk_copy(og_mine, og_theirs, og_send, og_recv, f).wait_send()
        chunk_copy(p_mine, p_theirs, p_send, p_recv, f).wait_send()
        return 0

    lax.fori_loop(0, 2 * zs, send_done, 0)
    hg_copy(tn).wait_send()

    @pl.when(z < zs - 1)
    def _():
        w_copy(fs, h, 0, above).wait_send()

    @pl.when(z > 0)
    def _():
        w_copy(fs, h, 1, below).wait_send()

    w_copy(fs, h, 3, other_core).wait_send()
    w_copy(fs, o, 3, other_core).wait_send()

    def relay_done(s, _):
        for way in range(2):
            zz = z - s + 2 * s * way
            nxt = z + 1 - 2 * way
            f = 2 * zz + core

            @pl.when((zz >= 0) & (zz < zs))
            def _():
                @pl.when((nxt >= 0) & (nxt < zs))
                def _():
                    w_copy(f, h, way, above if way == 0 else below).wait_send()

                w_copy(f, h, 2, other_dp).wait_send()
                w_copy(f, h, 3, other_core).wait_send()
                w_copy(f, o, 3, other_core).wait_send()

        return 0

    lax.fori_loop(1, zs, relay_done, 0)


def chains(cols, targets):
    flat = cols.reshape(-1)
    count = flat.shape[0]
    spot = jnp.arange(count, dtype=jnp.int32)
    want = jnp.concatenate([flat, jnp.arange(targets, dtype=jnp.int32)])
    limit = jnp.concatenate([spot, jnp.full((targets,), count, jnp.int32)])
    same = (want[:, None] == flat[None, :]) & (spot[None, :] < limit[:, None])
    found = jnp.max(jnp.where(same, spot[None, :], -1), axis=1)
    return jnp.where(found < 0, count, found)


def local(
    attn_out,
    cotangent,
    old_weights,
    depth_coef,
    depth_pick,
    in_blocks,
    in_cols,
    out_blocks,
    out_cols,
):
    tok = attn_out.shape[0]
    fsdp = lax.axis_size("fsdp")
    tensor = lax.axis_size("tensor")
    dps = lax.axis_size("dp")
    zs = fsdp // 2
    _, feats, shard = old_weights.shape
    n_out = fsdp * shard // HEAD
    n_in = tensor * feats // HEAD
    rows_all, k_in = in_cols.shape
    rows_out, k_out = out_cols.shape
    rows_in = rows_all // tensor
    pairs_in, pairs_out = rows_all * k_in, rows_out * k_out
    n_terms = pairs_out + rows_in * k_in
    depth_k = depth_pick.shape[0]
    smem = pl.BlockSpec(memory_space=pltpu.SMEM)
    vmem = pl.BlockSpec(memory_space=pltpu.VMEM)
    dma = pltpu.SemaphoreType.DMA
    blocks = (n_out, tok, HEAD)
    grown, gattn, terms = pl.pallas_call(
        functools.partial(kernel, (zs, depth_k, k_in, k_out)),
        out_shape=(
            jax.ShapeDtypeStruct((tok, rows_out * HEAD), BF16),
            jax.ShapeDtypeStruct((tok, rows_in * HEAD), BF16),
            jax.ShapeDtypeStruct((n_terms, HEAD, HEAD), BF16),
        ),
        in_specs=[smem] * 6 + [vmem] * 5,
        out_specs=(vmem, vmem, vmem),
        scratch_shapes=[
            pltpu.VMEM((fsdp, feats, shard), BF16),
            pltpu.VMEM((max(pairs_in, pairs_out) + 1, tok, HEAD), F32),
            pltpu.VMEM(blocks, BF16),
            pltpu.VMEM(blocks, BF16),
            pltpu.VMEM(blocks, BF16),
            pltpu.VMEM(blocks, BF16),
            pltpu.VMEM(blocks, BF16),
            pltpu.VMEM((tok, feats), BF16),
            pltpu.VMEM((tok, feats), F32),
            pltpu.VMEM((n_in, tok, HEAD), BF16),
            dma((fsdp, 2, 4)),
            dma((fsdp, 2)),
            dma((fsdp,)),
            dma((fsdp,)),
            dma((fsdp,)),
            dma((fsdp,)),
            dma,
            dma,
        ],
        compiler_params=pltpu.CompilerParams(
            collective_id=0, has_side_effects=True, vmem_limit_bytes=52 * 2**20
        ),
    )(
        depth_pick,
        depth_coef,
        in_cols.reshape(-1),
        out_cols.reshape(-1),
        chains(in_cols, n_in),
        chains(out_cols, n_out),
        attn_out,
        cotangent,
        old_weights,
        in_blocks.reshape(pairs_in, HEAD, HEAD),
        out_blocks.reshape(pairs_out, HEAD, HEAD),
    )
    total = lax.psum(terms, ("dp", "fsdp")).astype(F32)
    total = total * float(tok * dps * fsdp) ** (-0.5)
    out_sum = total[:pairs_out].reshape(rows_out, k_out, HEAD, HEAD)
    in_sum = total[pairs_out:].reshape(rows_in, k_in, HEAD, HEAD)
    return grown, gattn, in_sum, out_sum


def solution(mesh):
    placed = (
        P(("dp", "fsdp"), None),
        P(("dp", "fsdp"), "tensor"),
        P(None, "tensor", "fsdp"),
        P(),
        P(),
        P(),
        P(),
        P("tensor", None, None, None),
        P("tensor", None),
    )
    return jax.shard_map(
        local,
        mesh=mesh,
        in_specs=placed,
        out_specs=(
            P(("dp", "fsdp"), "tensor"),
            P(("dp", "fsdp"), "tensor"),
            P("tensor", None, None, None),
            P("tensor", None, None, None),
        ),
        check_vma=False,
    )
```

time: 318 us -> 205 us (0.64)
  waiting for transfers between devices: 225 us -> 106 us
  Pallas kernels: 0 us -> 69.8 us
  matrix products: 28 us -> 0 us
  local copies, waits for them, and re-layouts: 27.2 us -> 8.49 us
  blocking collectives: 8.03 us -> 0 us
  other arithmetic: 8.15 us -> 3.71 us
  between operations: 17.8 us -> 14.1 us
    pallas_call x0 -> x1, Pallas kernels: none -> 69.8 us  [local(): pl.pallas_call(functools.partial(kernel, (zs, depth_k, k_in, k_out)), out...]
    all_gather x1 -> x0, waiting for transfers between devices: 60.1 us -> none  [gathered_mix(): return lax.all_gather(mixed_weight, 'fsdp', axis=1, tiled=True)]
    psum x2 -> x1, waiting for transfers between devices: 165 us -> 106 us  [local(): total = lax.psum(terms, ('dp', 'fsdp')).astype(F32)]
    dot_general x10 -> x0, matrix products: 28 us -> none  [the longest x1 6.62 us: local(): jnp.einsum('to,fo->tf', old_grad, full_mix, preferred_element_type=jnp.fl...]
    all_gather x1 -> x0, blocking collectives: 8.03 us -> none  [local(): lax.all_gather(hidden_grad_local, 'tensor', axis=1, tiled=True)]
    dot_general x2 -> x0, local copies, waits for them, and re-layouts: 7.34 us -> none  [the longest x1 3.71 us: local(): jnp.einsum('tre,rkde->trkd', cot_blocks, out_blocks, preferred_element_ty...]
    gather x4 -> x0, local copies, waits for them, and re-layouts: 6.59 us -> none  [the longest x2 4.83 us: local(): jnp.take(old_out.reshape(tok_rows, BO_OLD, HEAD), out_cols, axis=1)]
    convert_element_type x1 -> x0, other arithmetic: 4.21 us -> none  [local(): mixed_weight = mixed_weight.astype(jnp.bfloat16)]
  transfers between devices with their start and end apart: 3 -> 1, of which waited for: 3 -> 1; matrix products, arithmetic and copies ran while one was open for 9% -> 0% of each run, Pallas kernels for 0% -> 0%
where the time goes in v1:
time: 205 us; the launch traced here: 202 us
  waiting for transfers between devices  106 us (52%)
  Pallas kernels  69.8 us (34%)
  between operations  14.1 us (7%)
  local copies, waits for them, and re-layouts  8.49 us (4%)
  other arithmetic  3.71 us (2%)
    psum x1, waiting for transfers between devices, local(): total = lax.psum(terms, ('dp', 'fsdp')).astype(F32)  106 us
    pallas_call x1, Pallas kernels, local(): pl.pallas_call(functools.partial(kernel, (zs, depth_k, k_in, k_out)), out...  69.8 us
    unnamed x10, local copies, waits for them, and re-layouts  5.49 us
  transfers between devices with their start and end apart: 1, of which 1 were waited for; matrix products, arithmetic and copies ran while one was open for 0% of the time, Pallas kernels for 0%

profile of v1, /device:TPU:9, one launch (start us, length us, event | category | flops | bytes accessed | tf_op | source)
XLA Modules:
  0.0 202.1 jit_solution(1468955293659697081)
XLA Ops:
  7.2 0.0 all-reduce.2.cloned.1.call-start
  7.2 0.8 copy.17
  8.0 0.1 reshape.34.in_cols
  8.1 0.1 pad_add_fusion
  8.2 0.7 select_reduce_fusion.1
  8.9 0.8 copy.18
  9.7 0.1 reshape.35.out_cols
  9.8 0.1 pad_add_fusion.1
  9.9 0.7 select_reduce_fusion
  10.6 0.0 copy-start
  10.6 1.1 copy-done
  11.7 0.0 copy-start.1
  11.7 0.7 copy-done.1
  12.4 0.0 copy-start.2
  12.4 0.7 copy-done.2
  13.0 69.8 %shard_map.120 = (bf16[128,2560]{1,0:T(8,128)(2,1)S(1)}, bf16[128,1280]{1,0:T(8,128)(2,1)S(1)}, bf16[60,128,128]{2,1,0:T(8,128)(2,1)}) custom-call(s32[2]{0:T(128)S(1)} %copy-done.1, f32[2]{0:T(128)S(1)} %copy-done.2, s32[40]{0:T(128)S(1)} %reshape.34.in_cols, s32[40]{0:T(128)S(1)} %reshape.35.out_cols, s32[56]{0:T(128)S(1)} %compare_select_fusion.1.in_ptr, ...), custom_call_target="tpu_custom_call" | custom-call | tf_op jit(solution)/shard_map/pallas_call | solution.py:395
  82.8 0.0 all-reduce.2.cloned.1.call-update
  82.9 106.0 %all-reduce.2.cloned.1.call-done = bf16[60,128,128]{2,1,0:T(8,128)(2,1)} async-done(((bf16[60,128,128]{2,1,0:T(8,128)(2,1)}), bf16[60,128,128]{2,1,0:T(8,128)(2,1)}) %all-reduce.2.cloned.1.call-update) | async-done | bytes 1966096 | tf_op jit(solution)/shard_map/psum | solution.py:440
  188.8 2.1 %convert_multiply_fusion = f32[60,128,128]{2,1,0:T(8,128)S(1)} fusion(bf16[60,128,128]{2,1,0:T(8,128)(2,1)} %all-reduce.2.cloned.1.call-done), kind=kLoop, calls=%fused_computation | loop fusion | flops 1966080 | bytes 5898240 | tf_op jit(solution)/shard_map/mul | solution.py:441
  190.9 1.1 slice.8
  192.0 1.7 slice.9
  193.7 0.8 copy.22
  194.5 0.7 copy.23
  (4 shorter events, 0.0 us)
Async XLA Ops:
  7.2 181.7 %all-reduce.2.cloned.1.call-start = ((), (), s32[]{:S(2)}) async-start(), calls=%async_computation | async-start | bytes 3932160 | tf_op jit(solution)/shard_map/psum | solution.py:440
  10.6 1.1 copy-start
  11.7 0.7 copy-start.1
  12.4 0.7 copy-start.2
Sparse Core Ops, SparseCore 0:
  83.0 105.8 all-reduce.1

commit v2 on v1

--- a/solution.py
+++ b/solution.py
@@ -32,7 +32,8 @@
     out_b,
     grown,
     gattn,
-    terms,
+    out_sum,
+    in_sum,
     w_all,
     sums,
     og_mine,
@@ -51,8 +52,10 @@
     p_recv,
     hg_send,
     hg_recv,
+    *streams,
 ):
-    zs, depth_k, k_in, k_out = dims
+    zs, dps, depth_k, k_in, k_out, scale = dims
+    streams = (streams[:14], streams[14:])
     shard = w_all.shape[2]
     feats = w_all.shape[1]
     half_rows = feats // 2
@@ -115,19 +118,15 @@
         )
 
     barrier = pltpu.get_barrier_semaphore()
-    for to in (other_core, other_dp, other_tn):
+    for to in (other_core, other_tn):
         pl.semaphore_signal(barrier, inc=1, device_id=to, device_id_type=MESH)
-
-    @pl.when(z > 0)
-    def _():
-        pl.semaphore_signal(barrier, inc=1, device_id=below, device_id_type=MESH)
-
-    @pl.when(z < zs - 1)
-    def _():
-        pl.semaphore_signal(barrier, inc=1, device_id=above, device_id_type=MESH)
-
-    inner = (z > 0).astype(jnp.int32) + (z < zs - 1).astype(jnp.int32)
-    pl.semaphore_wait(barrier, 3 + inner)
+    for i in range(1, dps):
+        to = {"dp": (dp + i) % dps}
+        pl.semaphore_signal(barrier, inc=1, device_id=to, device_id_type=MESH)
+    for i in range(1, zs):
+        to = {"fsdp": 2 * ((z + i) % zs) + core}
+        pl.semaphore_signal(barrier, inc=1, device_id=to, device_id_type=MESH)
+    pl.semaphore_wait(barrier, dps + zs)
 
     mix_rows = 64
 
@@ -270,6 +269,187 @@
         hg_all[tn * nl + b] = hg_acc[:, b * HEAD : (b + 1) * HEAD].astype(BF16)
     hg_copy(tn).start()
 
+    def piece_copy(src, dst, send, recv, to):
+        return pltpu.make_async_remote_copy(
+            src_ref=src, dst_ref=dst, send_sem=send, recv_sem=recv, device_id=to, device_id_type=MESH
+        )
+
+    class Stream:
+        def __init__(self, refs):
+            (self.g, self.from_core, self.from_dp, self.from_z, self.full) = refs[:5]
+            (self.c_s, self.c_r, self.y_s, self.y_r, self.z_s, self.z_r) = refs[5:11]
+            (self.a_r, self.az_s, self.ay_s) = refs[11:14]
+            self.u = self.from_z.shape[1]
+
+        def rows(self, c, e, q):
+            return pl.ds(pl.multiple_of(((c * dps + e) * zs + q) * self.u, self.u), self.u)
+
+        def core_copy(self, e, q):
+            return piece_copy(
+                self.g.at[self.rows(1 - core, e, q)],
+                self.from_core.at[e * zs + q],
+                self.c_s.at[e, q],
+                self.c_r.at[e, q],
+                other_core,
+            )
+
+        def dp_copy(self, src, e, q):
+            return piece_copy(
+                self.g.at[self.rows(core, e, q)],
+                self.from_dp.at[src * zs + q],
+                self.y_s.at[e, q],
+                self.y_r.at[src, q],
+                {"dp": e},
+            )
+
+        def z_copy(self, src, q):
+            return piece_copy(
+                self.g.at[self.rows(core, dp, q)],
+                self.from_z.at[src],
+                self.z_s.at[q],
+                self.z_r.at[src],
+                {"fsdp": 2 * q + core},
+            )
+
+        def full_copy(self, c, e, q, send, to):
+            piece = self.full.at[self.rows(c, e, q)]
+            return piece_copy(piece, piece, send, self.a_r.at[c, e, q], to)
+
+        def gather_z(self, q):
+            return self.full_copy(core, dp, z, self.az_s.at[q], {"fsdp": 2 * q + core})
+
+        def gather_dp(self, e, q):
+            return self.full_copy(core, dp, q, self.ay_s.at[e, q], {"dp": e})
+
+        def gather_core(self, e, q):
+            return self.full_copy(core, e, q, self.c_s.at[e, q], other_core)
+
+        def came(self, c, e, q):
+            self.full_copy(c, e, q, self.c_s.at[e, q], other_core).wait_recv()
+
+        def each_q(self, body):
+            def one(i, _):
+                body((z + 1 + i) % zs)
+                return 0
+
+            lax.fori_loop(0, zs, one, 0)
+
+        def each_e(self, body, own=False):
+            def one(i, _):
+                body((dp + 1 + i) % dps)
+                return 0
+
+            lax.fori_loop(0, dps if own else dps - 1, one, 0)
+
+        def start_core(self):
+            self.each_e(lambda e: self.each_q(lambda q: self.core_copy(e, q).start()), True)
+
+        def core_sums(self):
+            def one(e, q):
+                self.core_copy(e, q).wait()
+                rows = self.rows(core, e, q)
+                total = self.g[rows, :].astype(F32) + self.from_core[e * zs + q].astype(F32)
+                self.g[rows, :] = total.astype(BF16)
+
+                @pl.when(e != dp)
+                def _():
+                    self.dp_copy(dp, e, q).start()
+
+            self.each_e(lambda e: self.each_q(lambda q: one(e, q)), True)
+
+        def dp_sums(self):
+            def one(q):
+                rows = self.rows(core, dp, q)
+                total = self.g[rows, :].astype(F32)
+                for i in range(1, dps):
+                    src = (dp + i) % dps
+                    self.dp_copy(src, dp, q).wait_recv()
+                    total = total + self.from_dp[src * zs + q].astype(F32)
+                self.g[rows, :] = total.astype(BF16)
+
+                @pl.when(q != z)
+                def _():
+                    self.z_copy(z, q).start()
+
+            self.each_q(one)
+
+        def z_sums(self):
+            total = self.g[self.rows(core, dp, z), :].astype(F32)
+            for i in range(1, zs):
+                src = (z + i) % zs
+                self.z_copy(src, z).wait_recv()
+                total = total + self.from_z[src].astype(F32)
+            self.full[self.rows(core, dp, z), :] = total.astype(BF16)
+
+            def to_z(i, _):
+                self.gather_z((z + i) % zs).start()
+                return 0
+
+            lax.fori_loop(1, zs, to_z, 0)
+            self.each_e(lambda e: self.gather_dp(e, z).start())
+            self.gather_core(dp, z).start()
+
+        def near(self, body):
+            def one(s, _):
+                for zz in (z - s, z + s):
+                    @pl.when((zz >= 0) & (zz < zs))
+                    def _():
+                        body(zz)
+
+                return 0
+
+            lax.fori_loop(1, zs, one, 0)
+
+        def forward_z(self):
+            def one(q):
+                self.came(core, dp, q)
+                self.each_e(lambda e: self.gather_dp(e, q).start())
+                self.gather_core(dp, q).start()
+
+            self.near(one)
+
+        def forward_dp(self):
+            def one(q):
+                def each(e):
+                    self.came(core, e, q)
+                    self.gather_core(e, q).start()
+
+                self.each_e(each)
+
+            one(z)
+            self.near(one)
+
+        def finish(self, result):
+            self.each_e(lambda e: self.each_q(lambda q: self.came(1 - core, e, q)), True)
+
+            def block(i, _):
+                rows = pl.ds(pl.multiple_of(i * HEAD, HEAD), HEAD)
+                result[i] = self.full[rows, :].astype(F32) * scale
+                return 0
+
+            lax.fori_loop(0, result.shape[0], block, 0)
+
+        def drain(self):
+            self.each_e(lambda e: self.each_q(lambda q: self.dp_copy(dp, e, q).wait_send()))
+            self.each_e(lambda e: self.each_q(lambda q: self.gather_dp(e, q).wait_send()))
+            self.each_e(lambda e: self.each_q(lambda q: self.gather_core(e, q).wait_send()), True)
+
+            def to_z(i, _):
+                self.z_copy(z, (z + i) % zs).wait_send()
+                self.gather_z((z + i) % zs).wait_send()
+                return 0
+
+            lax.fori_loop(1, zs, to_z, 0)
+
+        def clear_tail(self, used):
+            spare = self.g.shape[0] - used
+            if spare > 0:
+                self.g[used:, :] = jnp.zeros((spare, HEAD), BF16)
+
+    outs, ins = Stream(streams[0]), Stream(streams[1])
+    outs.clear_tail(pairs_out * HEAD)
+    ins.clear_tail(rows_in * k_in * HEAD)
+
     def add_shard(f, _):
         chunk_copy(p_mine, p_theirs, p_send, p_recv, f).wait_recv()
         for b in range(nb):
@@ -282,35 +462,65 @@
 
     def out_row(r, _):
         cols = pl.ds(pl.multiple_of(r * HEAD, HEAD), HEAD)
+        for k in range(k_out):
+            j = r * k_out + k
+            to = pl.ds(pl.multiple_of(j * HEAD, HEAD), HEAD)
+            outs.g[to, :] = dot(oo[out_cols[j]], cot[:, cols], 0, 0).astype(BF16)
+        return 0
+
+    lax.fori_loop(0, rows_out, out_row, 0, unroll=4)
+    outs.start_core()
+    hg_copy(1 - tn).wait_recv()
+
+    def in_row(r, _):
+        mine = tn * rows_in + r
+        mine_cols = pl.ds(pl.multiple_of(mine * HEAD, HEAD), HEAD)
+        for k in range(k_in):
+            block = hg_all[in_cols[mine * k_in + k]]
+            to = pl.ds(pl.multiple_of((r * k_in + k) * HEAD, HEAD), HEAD)
+            ins.g[to, :] = dot(attn[:, mine_cols], block, 0, 0).astype(BF16)
+        return 0
+
+    lax.fori_loop(0, rows_in, in_row, 0, unroll=2)
+    ins.start_core()
+    outs.core_sums()
+    ins.core_sums()
+
+    def grown_row(r, _):
+        cols = pl.ds(pl.multiple_of(r * HEAD, HEAD), HEAD)
         total = None
         for k in range(k_out):
             j = r * k_out + k
-            block = oo[out_cols[j]]
-            term = dot(block, out_b[j])
+            term = dot(oo[out_cols[j]], out_b[j])
             total = term if total is None else total + term
-            terms[j] = dot(block, cot[:, cols], 0, 0).astype(BF16)
         grown[:, cols] = total.astype(BF16)
         return 0
 
-    lax.fori_loop(0, rows_out, out_row, 0, unroll=4)
-
-    hg_copy(1 - tn).wait_recv()
-
-    def in_row(r, _):
+    lax.fori_loop(0, rows_out, grown_row, 0, unroll=4)
+    outs.dp_sums()
+
+    def gattn_row(r, _):
         cols = pl.ds(pl.multiple_of(r * HEAD, HEAD), HEAD)
-        mine = tn * rows_in + r
-        mine_cols = pl.ds(pl.multiple_of(mine * HEAD, HEAD), HEAD)
         total = None
         for k in range(k_in):
-            j = mine * k_in + k
-            block = hg_all[in_cols[j]]
-            term = dot(block, in_b[j], 1, 1)
+            j = (tn * rows_in + r) * k_in + k
+            term = dot(hg_all[in_cols[j]], in_b[j], 1, 1)
             total = term if total is None else total + term
-            terms[pairs_out + r * k_in + k] = dot(attn[:, mine_cols], block, 0, 0).astype(BF16)
         gattn[:, cols] = total.astype(BF16)
         return 0
 
-    lax.fori_loop(0, rows_in, in_row, 0, unroll=2)
+    lax.fori_loop(0, rows_in, gattn_row, 0, unroll=2)
+    ins.dp_sums()
+    outs.z_sums()
+    ins.z_sums()
+    outs.forward_z()
+    ins.forward_z()
+    outs.forward_dp()
+    ins.forward_dp()
+    outs.finish(out_sum)
+    ins.finish(in_sum)
+    outs.drain()
+    ins.drain()
 
     def send_done(f, _):
         chunk_copy(og_mine, og_theirs, og_send, og_recv, f).wait_send()
@@ -386,21 +596,42 @@
     rows_out, k_out = out_cols.shape
     rows_in = rows_all // tensor
     pairs_in, pairs_out = rows_all * k_in, rows_out * k_out
-    n_terms = pairs_out + rows_in * k_in
     depth_k = depth_pick.shape[0]
     smem = pl.BlockSpec(memory_space=pltpu.SMEM)
     vmem = pl.BlockSpec(memory_space=pltpu.VMEM)
     dma = pltpu.SemaphoreType.DMA
     blocks = (n_out, tok, HEAD)
-    grown, gattn, terms = pl.pallas_call(
-        functools.partial(kernel, (zs, depth_k, k_in, k_out)),
+    scale = float(tok * dps * fsdp) ** (-0.5)
+
+    def stream_scratch(rows):
+        u = -(-rows // (2 * dps * zs * 16)) * 16
+        return [
+            pltpu.VMEM((2 * dps * zs * u, HEAD), BF16),
+            pltpu.VMEM((dps * zs, u, HEAD), BF16),
+            pltpu.VMEM((dps * zs, u, HEAD), BF16),
+            pltpu.VMEM((zs, u, HEAD), BF16),
+            pltpu.VMEM((2 * dps * zs * u, HEAD), BF16),
+            dma((dps, zs)),
+            dma((dps, zs)),
+            dma((dps, zs)),
+            dma((dps, zs)),
+            dma((zs,)),
+            dma((zs,)),
+            dma((2, dps, zs)),
+            dma((zs,)),
+            dma((dps, zs)),
+        ]
+
+    grown, gattn, out_sum, in_sum = pl.pallas_call(
+        functools.partial(kernel, (zs, dps, depth_k, k_in, k_out, scale)),
         out_shape=(
             jax.ShapeDtypeStruct((tok, rows_out * HEAD), BF16),
             jax.ShapeDtypeStruct((tok, rows_in * HEAD), BF16),
-            jax.ShapeDtypeStruct((n_terms, HEAD, HEAD), BF16),
+            jax.ShapeDtypeStruct((pairs_out, HEAD, HEAD), F32),
+            jax.ShapeDtypeStruct((rows_in * k_in, HEAD, HEAD), F32),
         ),
         in_specs=[smem] * 6 + [vmem] * 5,
-        out_specs=(vmem, vmem, vmem),
+        out_specs=(vmem, vmem, vmem, vmem),
         scratch_shapes=[
             pltpu.VMEM((fsdp, feats, shard), BF16),
             pltpu.VMEM((max(pairs_in, pairs_out) + 1, tok, HEAD), F32),
@@ -420,6 +651,8 @@
             dma((fsdp,)),
             dma,
             dma,
+            *stream_scratch(pairs_out * HEAD),
+            *stream_scratch(rows_in * k_in * HEAD),
         ],
         compiler_params=pltpu.CompilerParams(
             collective_id=0, has_side_effects=True, vmem_limit_bytes=52 * 2**20
@@ -437,10 +670,8 @@
         in_blocks.reshape(pairs_in, HEAD, HEAD),
         out_blocks.reshape(pairs_out, HEAD, HEAD),
     )
-    total = lax.psum(terms, ("dp", "fsdp")).astype(F32)
-    total = total * float(tok * dps * fsdp) ** (-0.5)
-    out_sum = total[:pairs_out].reshape(rows_out, k_out, HEAD, HEAD)
-    in_sum = total[pairs_out:].reshape(rows_in, k_in, HEAD, HEAD)
+    in_sum = in_sum.reshape(rows_in, k_in, HEAD, HEAD)
+    out_sum = out_sum.reshape(rows_out, k_out, HEAD, HEAD)
     return grown, gattn, in_sum, out_sum
 
 

time: 205 us -> 125 us (0.61); the launches traced: 202 us -> 125 us
  waiting for transfers between devices: 106 us -> 0 us
  Pallas kernels: 69.8 us -> 113 us
  between operations: 14.1 us -> 0.69 us
    psum x1 -> x0, waiting for transfers between devices: 106 us -> none  [local(): total = lax.psum(terms, ('dp', 'fsdp')).astype(F32)]
    pallas_call x1, Pallas kernels: 69.8 us -> 113 us  [local(): pl.pallas_call(functools.partial(kernel, (zs, dps, depth_k, k_in, k_out,...]
    unnamed x10 -> x16, local copies, waits for them, and re-layouts: 5.49 us -> 9.21 us
    slice x2 -> x0, local copies, waits for them, and re-layouts: 2.82 us -> none  [the longest x1 1.67 us: local(): out_sum = total[:pairs_out].reshape(rows_out, k_out, HEAD, HEAD)]
    mul x1 -> x0, other arithmetic: 2.05 us -> none  [local(): total = total * float(tok * dps * fsdp) ** (-0.5)]
  transfers between devices with their start and end apart: 1 -> 0, of which waited for: 1 -> 0; matrix products, arithmetic and copies ran while one was open for 0% -> 0% of each run, Pallas kernels for 0% -> 0%
where the time goes in v2:
time: 125 us
  Pallas kernels  113 us (90%)
  local copies, waits for them, and re-layouts  9.39 us (8%)
  other arithmetic  1.67 us (1%)
    pallas_call x1, Pallas kernels, local(): pl.pallas_call(functools.partial(kernel, (zs, dps, depth_k, k_in, k_out,...  113 us
    unnamed x16, local copies, waits for them, and re-layouts  9.21 us

profile of v2, /device:TPU:9, one launch (start us, length us, event | category | flops | bytes accessed | tf_op | source)
XLA Modules:
  0.0 124.8 jit_solution(3087223259517673147)
XLA Ops:
  0.6 0.8 copy.17
  1.4 0.1 reshape.34.in_cols
  1.5 0.1 pad_add_fusion
  1.6 0.8 select_reduce_fusion.1
  2.4 0.8 copy.18
  3.1 0.1 reshape.35.out_cols
  3.2 0.1 pad_add_fusion.1
  3.3 0.8 select_reduce_fusion
  4.1 0.0 copy-start
  4.1 1.1 copy-done
  5.1 0.0 copy-start.1
  5.1 0.7 copy-done.1
  5.8 0.0 copy-start.2
  5.8 0.7 copy-done.2
  6.5 113.0 %shard_map.120 = (bf16[128,2560]{1,0:T(8,128)(2,1)S(1)}, bf16[128,1280]{1,0:T(8,128)(2,1)S(1)}, f32[40,128,128]{2,1,0:T(8,128)}, f32[20,128,128]{2,1,0:T(8,128)}) custom-call(s32[2]{0:T(128)S(1)} %copy-done.1, f32[2]{0:T(128)S(1)} %copy-done.2, s32[40]{0:T(128)S(1)} %reshape.34.in_cols, s32[40]{0:T(128)S(1)} %reshape.35.out_cols, ...), custom_call_target="tpu_custom_call" | custom-call | tf_op jit(solution)/shard_map/pallas_call | solution.py:625
  119.5 0.0 copy-start.4
  119.5 0.8 copy.23
  120.3 0.7 copy.24
  121.1 0.0 copy-done.4
  121.1 0.0 copy-start.3
  121.1 1.1 copy.25
  122.1 1.2 copy-done.3
  123.3 1.5 %copy.26 = f32[20,2,128,128]{3,2,1,0:T(8,128)} copy(f32[20,2,128,128]{3,2,1,0:T(8,128)S(1)} %bitcast.4) | data formatting | bytes 5242880
  (4 shorter events, 0.0 us)
Async XLA Ops:
  4.1 1.1 copy-start
  5.1 0.7 copy-start.1
  5.8 0.7 copy-start.2
  119.5 1.6 %copy-start.4 = (f32[20,128,128]{2,1,0:T(8,128)S(1)}, f32[20,128,128]{2,1,0:T(8,128)}, u32[]{:S(2)}) copy-start(f32[20,128,128]{2,1,0:T(8,128)} %get-tuple-element.10) | copy-start | bytes 3932164
  121.1 2.2 %copy-start.3 = (f32[40,128,128]{2,1,0:T(8,128)S(1)}, f32[40,128,128]{2,1,0:T(8,128)}, u32[]{:S(2)}) copy-start(f32[40,128,128]{2,1,0:T(8,128)} %get-tuple-element.11) | copy-start | bytes 7864324

commit v3 on v2

--- a/solution.py
+++ b/solution.py
@@ -19,21 +19,24 @@
 
 def kernel(
     dims,
-    pick,
+    table,
     coef,
-    in_cols,
-    out_cols,
-    in_ptr,
-    out_ptr,
+    attn_hbm,
+    cot_hbm,
+    old_w_hbm,
+    in_b_hbm,
+    out_b_hbm,
+    grown,
+    gattn,
+    out_full,
+    in_full,
     attn,
     cot,
-    old_w,
+    old_w_first,
+    old_w_last,
     in_b,
     out_b,
-    grown,
-    gattn,
-    out_sum,
-    in_sum,
+    load_sem,
     w_all,
     sums,
     og_mine,
@@ -54,18 +57,44 @@
     hg_recv,
     *streams,
 ):
-    zs, dps, depth_k, k_in, k_out, scale = dims
-    streams = (streams[:14], streams[14:])
+    zs, dps, depth_k, k_in, k_out, rows_all, rows_out, pairs, n_sub = dims
+    streams = (streams[:13], streams[13:])
     shard = w_all.shape[2]
     feats = w_all.shape[1]
     half_rows = feats // 2
     nb = shard // HEAD
     nl = feats // HEAD
     n_out = og_mine.shape[0]
-    pairs_in = in_cols.shape[0]
-    pairs_out = out_cols.shape[0]
-    rows_all = pairs_in // k_in
-    rows_out = pairs_out // k_out
+    sub_rows = half_rows // n_sub
+    pairs_in = rows_all * k_in
+    pairs_out = rows_out * k_out
+    targets = (table.shape[0] - depth_k) // 2 - 2 * pairs
+
+    def in_col(r, k):
+        return table[depth_k + k * rows_all + r]
+
+    def out_col(r, k):
+        return table[depth_k + pairs + k * rows_out + r]
+
+    def in_link(i):
+        return table[depth_k + 2 * pairs + i]
+
+    def out_link(i):
+        return table[depth_k + 3 * pairs + targets + i]
+
+    def load(i, src, dst):
+        return pltpu.make_async_copy(src, dst, load_sem.at[i])
+
+    def load_mix(half, i, dst):
+        part = pl.ds(pl.multiple_of(half * half_rows, half_rows), half_rows)
+        return load(i, old_w_hbm.at[:, part], dst)
+
+    others = [
+        load(2, cot_hbm, cot),
+        load(3, out_b_hbm, out_b),
+        load(4, attn_hbm, attn),
+        load(5, in_b_hbm, in_b),
+    ]
     rows_in = gattn.shape[1] // HEAD
 
     dp = lax.axis_index("dp")
@@ -81,16 +110,21 @@
     above = {"fsdp": fs + 2}
     below = {"fsdp": fs - 2}
 
-    def rows_of(half):
-        return pl.ds(pl.multiple_of(half * half_rows, half_rows), half_rows)
-
-    def w_copy(f, half, kind, to):
-        piece = w_all.at[f, rows_of(half)]
+    load_first = load_mix(h, 0, old_w_first)
+    load_last = load_mix(o, 1, old_w_last)
+    load_first.start()
+    load_last.start()
+    for one_load in others:
+        one_load.start()
+
+    def w_copy(f, half, sub, kind, to):
+        start = pl.multiple_of(half * half_rows + sub * sub_rows, sub_rows)
+        piece = w_all.at[f, pl.ds(start, sub_rows)]
         return pltpu.make_async_remote_copy(
             src_ref=piece,
             dst_ref=piece,
-            send_sem=w_send.at[f, half, kind],
-            recv_sem=w_recv.at[f, half],
+            send_sem=w_send.at[f, half, sub, kind],
+            recv_sem=w_recv.at[f, half, sub],
             device_id=to,
             device_id_type=MESH,
         )
@@ -130,58 +164,76 @@
 
     mix_rows = 64
 
-    def mix(half):
+    def mix(half, old_w, sub):
         def body(i, _):
-            part = pl.ds(pl.multiple_of(half * half_rows + i * mix_rows, mix_rows), mix_rows)
-            total = coef[0] * old_w[pick[0], part, :].astype(F32)
+            start = sub * sub_rows + i * mix_rows
+            part = pl.ds(pl.multiple_of(start, mix_rows), mix_rows)
+            to = pl.ds(pl.multiple_of(half * half_rows + start, mix_rows), mix_rows)
+            total = coef[0] * old_w[table[0], part, :].astype(F32)
             for j in range(1, depth_k):
-                total = total + coef[j] * old_w[pick[j], part, :].astype(F32)
-            w_all[fs, part, :] = total.astype(BF16)
+                total = total + coef[j] * old_w[table[j], part, :].astype(F32)
+            w_all[fs, to, :] = total.astype(BF16)
             return 0
 
-        lax.fori_loop(0, half_rows // mix_rows, body, 0)
-
-    mix(h)
-
-    @pl.when(z < zs - 1)
-    def _():
-        w_copy(fs, h, 0, above).start()
-
-    @pl.when(z > 0)
-    def _():
-        w_copy(fs, h, 1, below).start()
-
-    w_copy(fs, h, 3, other_core).start()
-    mix(o)
-    w_copy(fs, o, 3, other_core).start()
-
-    sums[pairs_out] = jnp.zeros((HEAD, HEAD), F32)
+        lax.fori_loop(0, sub_rows // mix_rows, body, 0)
+
+    load_first.wait()
+
+    def first_half(q, _):
+        mix(h, old_w_first, q)
+
+        @pl.when(z < zs - 1)
+        def _():
+            w_copy(fs, h, q, 0, above).start()
+
+        @pl.when(z > 0)
+        def _():
+            w_copy(fs, h, q, 1, below).start()
+
+        w_copy(fs, h, q, 3, other_core).start()
+        return 0
+
+    lax.fori_loop(0, n_sub, first_half, 0)
+    load_last.wait()
+
+    def second_half(q, _):
+        mix(o, old_w_last, q)
+        w_copy(fs, o, q, 3, other_core).start()
+        return 0
+
+    lax.fori_loop(0, n_sub, second_half, 0)
+    others[0].wait()
+    others[1].wait()
+
+    sums[pairs] = jnp.zeros((HEAD, HEAD), F32)
 
     def back_row(r, _):
         cols = pl.ds(pl.multiple_of(r * HEAD, HEAD), HEAD)
         for k in range(k_out):
             j = r * k_out + k
-            sums[j] = dot(cot[:, cols], out_b[j], 1, 1) + sums[out_ptr[j]]
+            sums[j] = dot(cot[:, cols], out_b[j], 1, 1) + sums[out_link(k * rows_out + r)]
         return 0
 
     lax.fori_loop(0, rows_out, back_row, 0, unroll=4)
 
     def back_block(b, _):
-        og_mine[b] = sums[out_ptr[pairs_out + b]].astype(BF16)
+        og_mine[b] = sums[out_link(pairs + b)].astype(BF16)
         return 0
 
     lax.fori_loop(0, n_out, back_block, 0, unroll=4)
+
+    def shard_of(s, i, body):
+        zz = z - s + 2 * s * (i // 2)
+        cc = (core + i) % 2
+        live = (zz >= 0) & (zz < zs) & ((s > 0) | (i < 2))
+
+        @pl.when(live)
+        def _():
+            body(zz * 2 + cc, i % 2)
 
     def over_shards(s, body):
         def one(i, _):
-            zz = z - s + 2 * s * (i // 2)
-            cc = (core + i) % 2
-            live = (zz >= 0) & (zz < zs) & ((s > 0) | (i < 2))
-
-            @pl.when(live)
-            def _():
-                body(zz * 2 + cc, i % 2)
-
+            shard_of(s, i, body)
             return 0
 
         lax.fori_loop(0, 4, one, 0)
@@ -192,22 +244,23 @@
 
     lax.fori_loop(0, zs, og_start, 0)
 
-    sums[pairs_in] = jnp.zeros((HEAD, HEAD), F32)
+    others[2].wait()
+    others[3].wait()
 
     def hid_row(r, _):
         cols = pl.ds(pl.multiple_of(r * HEAD, HEAD), HEAD)
         for k in range(k_in):
             j = r * k_in + k
-            sums[j] = dot(attn[:, cols], in_b[j]) + sums[in_ptr[j]]
+            sums[j] = dot(attn[:, cols], in_b[j]) + sums[in_link(k * rows_all + r)]
         return 0
 
     lax.fori_loop(0, rows_all, hid_row, 0, unroll=4)
     for b in range(nl):
-        hid[:, b * HEAD : (b + 1) * HEAD] = sums[in_ptr[pairs_in + tn * nl + b]].astype(BF16)
+        hid[:, b * HEAD : (b + 1) * HEAD] = sums[in_link(pairs + tn * nl + b)].astype(BF16)
 
     hg_acc[...] = jnp.zeros_like(hg_acc)
 
-    def forward(f, s):
+    def forward(f):
         part = dot(hid[...], w_all[f]).astype(BF16)
         for b in range(nb):
             p_mine[f * nb + b] = part[:, b * HEAD : (b + 1) * HEAD]
@@ -221,7 +274,19 @@
         ]
         hg_acc[...] += dot(jnp.concatenate(blocks, axis=1), w_all[f], 1, 1)
 
-    def step(s, _):
+    def first(f, flip):
+        @pl.when(flip == 1)
+        def _():
+            def came(q, _):
+                w_copy(f, 0, q, 3, other_core).wait_recv()
+                w_copy(f, 1, q, 3, other_core).wait_recv()
+                return 0
+
+            lax.fori_loop(0, n_sub, came, 0)
+
+        forward(f)
+
+    def relay(s, q):
         for way in range(2):
             zz = z - s + 2 * s * way
             nxt = z + 1 - 2 * way
@@ -229,41 +294,46 @@
 
             @pl.when((zz >= 0) & (zz < zs))
             def _():
-                w_copy(f, h, way, other_dp).wait_recv()
+                w_copy(f, h, q, way, other_dp).wait_recv()
 
                 @pl.when((nxt >= 0) & (nxt < zs))
                 def _():
-                    w_copy(f, h, way, above if way == 0 else below).start()
-
-                w_copy(f, h, 2, other_dp).start()
-                w_copy(f, h, 3, other_core).start()
-
-        def first(f, flip):
-            @pl.when(flip == 1)
-            def _():
-                w_copy(f, 0, 3, other_core).wait_recv()
-                w_copy(f, 1, 3, other_core).wait_recv()
-
-            forward(f, s)
-
-        over_shards(s - 1, first)
-
+                    w_copy(f, h, q, way, above if way == 0 else below).start()
+
+                w_copy(f, h, q, 2, other_dp).start()
+                w_copy(f, h, q, 3, other_core).start()
+
+    def pass_on(s, q):
         for way in range(2):
             zz = z - s + 2 * s * way
             f = 2 * zz + core
 
-            @pl.when((zz >= 0) & (zz < zs))
+            @pl.when((zz >= 0) & (zz < zs) & (s > 0))
             def _():
-                w_copy(f, o, 2, other_dp).wait_recv()
-                w_copy(f, o, 3, other_core).start()
-
-        @pl.when(s >= 2)
-        def _():
-            over_shards(s - 2, backward)
-
-        return 0
-
-    lax.fori_loop(1, zs + 2, step, 0)
+                w_copy(f, o, q, 2, other_dp).wait_recv()
+                w_copy(f, o, q, 3, other_core).start()
+
+    def step(s, _):
+        def part(q, _):
+            relay(s, q)
+            pass_on(s - (q == 0).astype(jnp.int32), (q + n_sub - 1) % n_sub)
+            shard_of(s - 1, q, first)
+
+            @pl.when((s >= 2) & (s < zs))
+            def _():
+                shard_of(s - 1, q, backward)
+
+            @pl.when(s == 2)
+            def _():
+                shard_of(0, q, backward)
+
+            return 0
+
+        lax.fori_loop(0, n_sub, part, 0)
+        return 0
+
+    lax.fori_loop(1, zs + 1, step, 0)
+    over_shards(zs - 1, backward)
 
     for b in range(nl):
         hg_all[tn * nl + b] = hg_acc[:, b * HEAD : (b + 1) * HEAD].astype(BF16)
@@ -275,10 +345,11 @@
         )
 
     class Stream:
-        def __init__(self, refs):
-            (self.g, self.from_core, self.from_dp, self.from_z, self.full) = refs[:5]
-            (self.c_s, self.c_r, self.y_s, self.y_r, self.z_s, self.z_r) = refs[5:11]
-            (self.a_r, self.az_s, self.ay_s) = refs[11:14]
+        def __init__(self, refs, full):
+            (self.g, self.from_core, self.from_dp, self.from_z) = refs[:4]
+            (self.c_s, self.c_r, self.y_s, self.y_r, self.z_s, self.z_r) = refs[4:10]
+            (self.a_r, self.az_s, self.ay_s) = refs[10:13]
+            self.full = full
             self.u = self.from_z.shape[1]
 
         def rows(self, c, e, q):
@@ -419,15 +490,8 @@
             one(z)
             self.near(one)
 
-        def finish(self, result):
+        def finish(self):
             self.each_e(lambda e: self.each_q(lambda q: self.came(1 - core, e, q)), True)
-
-            def block(i, _):
-                rows = pl.ds(pl.multiple_of(i * HEAD, HEAD), HEAD)
-                result[i] = self.full[rows, :].astype(F32) * scale
-                return 0
-
-            lax.fori_loop(0, result.shape[0], block, 0)
 
         def drain(self):
             self.each_e(lambda e: self.each_q(lambda q: self.dp_copy(dp, e, q).wait_send()))
@@ -446,7 +510,7 @@
             if spare > 0:
                 self.g[used:, :] = jnp.zeros((spare, HEAD), BF16)
 
-    outs, ins = Stream(streams[0]), Stream(streams[1])
+    outs, ins = Stream(streams[0], out_full), Stream(streams[1], in_full)
     outs.clear_tail(pairs_out * HEAD)
     ins.clear_tail(rows_in * k_in * HEAD)
 
@@ -465,7 +529,7 @@
         for k in range(k_out):
             j = r * k_out + k
             to = pl.ds(pl.multiple_of(j * HEAD, HEAD), HEAD)
-            outs.g[to, :] = dot(oo[out_cols[j]], cot[:, cols], 0, 0).astype(BF16)
+            outs.g[to, :] = dot(oo[out_col(r, k)], cot[:, cols], 0, 0).astype(BF16)
         return 0
 
     lax.fori_loop(0, rows_out, out_row, 0, unroll=4)
@@ -476,7 +540,7 @@
         mine = tn * rows_in + r
         mine_cols = pl.ds(pl.multiple_of(mine * HEAD, HEAD), HEAD)
         for k in range(k_in):
-            block = hg_all[in_cols[mine * k_in + k]]
+            block = hg_all[in_col(mine, k)]
             to = pl.ds(pl.multiple_of((r * k_in + k) * HEAD, HEAD), HEAD)
             ins.g[to, :] = dot(attn[:, mine_cols], block, 0, 0).astype(BF16)
         return 0
@@ -491,7 +555,7 @@
         total = None
         for k in range(k_out):
             j = r * k_out + k
-            term = dot(oo[out_cols[j]], out_b[j])
+            term = dot(oo[out_col(r, k)], out_b[j])
             total = term if total is None else total + term
         grown[:, cols] = total.astype(BF16)
         return 0
@@ -504,7 +568,7 @@
         total = None
         for k in range(k_in):
             j = (tn * rows_in + r) * k_in + k
-            term = dot(hg_all[in_cols[j]], in_b[j], 1, 1)
+            term = dot(hg_all[in_col(tn * rows_in + r, k)], in_b[j], 1, 1)
             total = term if total is None else total + term
         gattn[:, cols] = total.astype(BF16)
         return 0
@@ -517,8 +581,8 @@
     ins.forward_z()
     outs.forward_dp()
     ins.forward_dp()
-    outs.finish(out_sum)
-    ins.finish(in_sum)
+    outs.finish()
+    ins.finish()
     outs.drain()
     ins.drain()
 
@@ -530,18 +594,24 @@
     lax.fori_loop(0, 2 * zs, send_done, 0)
     hg_copy(tn).wait_send()
 
-    @pl.when(z < zs - 1)
-    def _():
-        w_copy(fs, h, 0, above).wait_send()
-
-    @pl.when(z > 0)
-    def _():
-        w_copy(fs, h, 1, below).wait_send()
-
-    w_copy(fs, h, 3, other_core).wait_send()
-    w_copy(fs, o, 3, other_core).wait_send()
-
-    def relay_done(s, _):
+    def own_done(q, _):
+        @pl.when(z < zs - 1)
+        def _():
+            w_copy(fs, h, q, 0, above).wait_send()
+
+        @pl.when(z > 0)
+        def _():
+            w_copy(fs, h, q, 1, below).wait_send()
+
+        w_copy(fs, h, q, 3, other_core).wait_send()
+        w_copy(fs, o, q, 3, other_core).wait_send()
+        return 0
+
+    lax.fori_loop(0, n_sub, own_done, 0)
+
+    def relay_done(i, _):
+        s = 1 + i // n_sub
+        q = i % n_sub
         for way in range(2):
             zz = z - s + 2 * s * way
             nxt = z + 1 - 2 * way
@@ -551,26 +621,35 @@
             def _():
                 @pl.when((nxt >= 0) & (nxt < zs))
                 def _():
-                    w_copy(f, h, way, above if way == 0 else below).wait_send()
-
-                w_copy(f, h, 2, other_dp).wait_send()
-                w_copy(f, h, 3, other_core).wait_send()
-                w_copy(f, o, 3, other_core).wait_send()
-
-        return 0
-
-    lax.fori_loop(1, zs, relay_done, 0)
-
-
-def chains(cols, targets):
-    flat = cols.reshape(-1)
-    count = flat.shape[0]
-    spot = jnp.arange(count, dtype=jnp.int32)
-    want = jnp.concatenate([flat, jnp.arange(targets, dtype=jnp.int32)])
-    limit = jnp.concatenate([spot, jnp.full((targets,), count, jnp.int32)])
-    same = (want[:, None] == flat[None, :]) & (spot[None, :] < limit[:, None])
-    found = jnp.max(jnp.where(same, spot[None, :], -1), axis=1)
-    return jnp.where(found < 0, count, found)
+                    w_copy(f, h, q, way, above if way == 0 else below).wait_send()
+
+                w_copy(f, h, q, 2, other_dp).wait_send()
+                w_copy(f, h, q, 3, other_core).wait_send()
+                w_copy(f, o, q, 3, other_core).wait_send()
+
+        return 0
+
+    lax.fori_loop(0, (zs - 1) * n_sub, relay_done, 0)
+
+
+def index_table(pick, in_cols, out_cols, targets):
+    pairs = max(in_cols.size, out_cols.size)
+    flats, orders = [], []
+    for cols in (in_cols, out_cols):
+        rows, terms = cols.shape
+        short = (0, pairs - cols.size)
+        order = jnp.arange(rows, dtype=jnp.int32)[None, :] * terms
+        order = order + jnp.arange(terms, dtype=jnp.int32)[:, None]
+        flats.append(jnp.pad(cols.T.reshape(-1), short, constant_values=-1))
+        orders.append(jnp.pad(order.reshape(-1), short, constant_values=pairs))
+    flat, order = jnp.stack(flats), jnp.stack(orders)
+    named = jnp.broadcast_to(jnp.arange(targets, dtype=jnp.int32), (2, targets))
+    want = jnp.concatenate([flat, named], axis=1)
+    limit = jnp.concatenate([order, jnp.full((2, targets), pairs, jnp.int32)], axis=1)
+    same = (want[:, :, None] == flat[:, None, :]) & (order[:, None, :] < limit[:, :, None])
+    found = jnp.max(jnp.where(same, order[:, None, :], -1), axis=2)
+    found = jnp.where(found < 0, pairs, found)
+    return jnp.concatenate([pick, flat.reshape(-1), found.reshape(-1)])
 
 
 def local(
@@ -603,14 +682,19 @@
     blocks = (n_out, tok, HEAD)
     scale = float(tok * dps * fsdp) ** (-0.5)
 
+    n_sub = 4
+    pairs = max(pairs_in, pairs_out)
+
+    def stream_rows(rows):
+        return -(-rows // (2 * dps * zs * 16)) * 16
+
     def stream_scratch(rows):
-        u = -(-rows // (2 * dps * zs * 16)) * 16
+        u = stream_rows(rows)
         return [
             pltpu.VMEM((2 * dps * zs * u, HEAD), BF16),
             pltpu.VMEM((dps * zs, u, HEAD), BF16),
             pltpu.VMEM((dps * zs, u, HEAD), BF16),
             pltpu.VMEM((zs, u, HEAD), BF16),
-            pltpu.VMEM((2 * dps * zs * u, HEAD), BF16),
             dma((dps, zs)),
             dma((dps, zs)),
             dma((dps, zs)),
@@ -622,19 +706,39 @@
             dma((dps, zs)),
         ]
 
+    def stream_out(rows):
+        return jax.ShapeDtypeStruct((2 * dps * zs * stream_rows(rows), HEAD), BF16)
+
+    rows_o, rows_i = pairs_out * HEAD, rows_in * k_in * HEAD
+    arrays = (
+        attn_out,
+        cotangent,
+        old_weights,
+        in_blocks.reshape(pairs_in, HEAD, HEAD),
+        out_blocks.reshape(pairs_out, HEAD, HEAD),
+    )
     grown, gattn, out_sum, in_sum = pl.pallas_call(
-        functools.partial(kernel, (zs, dps, depth_k, k_in, k_out, scale)),
+        functools.partial(
+            kernel, (zs, dps, depth_k, k_in, k_out, rows_all, rows_out, pairs, n_sub)
+        ),
         out_shape=(
             jax.ShapeDtypeStruct((tok, rows_out * HEAD), BF16),
             jax.ShapeDtypeStruct((tok, rows_in * HEAD), BF16),
-            jax.ShapeDtypeStruct((pairs_out, HEAD, HEAD), F32),
-            jax.ShapeDtypeStruct((rows_in * k_in, HEAD, HEAD), F32),
+            stream_out(rows_o),
+            stream_out(rows_i),
         ),
-        in_specs=[smem] * 6 + [vmem] * 5,
+        in_specs=[smem] * 2 + [pl.BlockSpec(memory_space=pl.ANY)] * 5,
         out_specs=(vmem, vmem, vmem, vmem),
         scratch_shapes=[
+            pltpu.VMEM(attn_out.shape, BF16),
+            pltpu.VMEM(cotangent.shape, BF16),
+            pltpu.VMEM((old_weights.shape[0], feats // 2, shard), BF16),
+            pltpu.VMEM((old_weights.shape[0], feats // 2, shard), BF16),
+            pltpu.VMEM(arrays[3].shape, BF16),
+            pltpu.VMEM(arrays[4].shape, BF16),
+            dma((6,)),
             pltpu.VMEM((fsdp, feats, shard), BF16),
-            pltpu.VMEM((max(pairs_in, pairs_out) + 1, tok, HEAD), F32),
+            pltpu.VMEM((pairs + 1, tok, HEAD), F32),
             pltpu.VMEM(blocks, BF16),
             pltpu.VMEM(blocks, BF16),
             pltpu.VMEM(blocks, BF16),
@@ -643,35 +747,27 @@
             pltpu.VMEM((tok, feats), BF16),
             pltpu.VMEM((tok, feats), F32),
             pltpu.VMEM((n_in, tok, HEAD), BF16),
-            dma((fsdp, 2, 4)),
-            dma((fsdp, 2)),
+            dma((fsdp, 2, n_sub, 4)),
+            dma((fsdp, 2, n_sub)),
             dma((fsdp,)),
             dma((fsdp,)),
             dma((fsdp,)),
             dma((fsdp,)),
             dma,
             dma,
-            *stream_scratch(pairs_out * HEAD),
-            *stream_scratch(rows_in * k_in * HEAD),
+            *stream_scratch(rows_o),
+            *stream_scratch(rows_i),
         ],
         compiler_params=pltpu.CompilerParams(
             collective_id=0, has_side_effects=True, vmem_limit_bytes=52 * 2**20
         ),
     )(
-        depth_pick,
+        index_table(depth_pick, in_cols, out_cols, max(n_in, n_out)),
         depth_coef,
-        in_cols.reshape(-1),
-        out_cols.reshape(-1),
-        chains(in_cols, n_in),
-        chains(out_cols, n_out),
-        attn_out,
-        cotangent,
-        old_weights,
-        in_blocks.reshape(pairs_in, HEAD, HEAD),
-        out_blocks.reshape(pairs_out, HEAD, HEAD),
+        *arrays,
     )
-    in_sum = in_sum.reshape(rows_in, k_in, HEAD, HEAD)
-    out_sum = out_sum.reshape(rows_out, k_out, HEAD, HEAD)
+    in_sum = in_sum[:rows_i].reshape(rows_in, k_in, HEAD, HEAD).astype(F32) * scale
+    out_sum = out_sum[:rows_o].reshape(rows_out, k_out, HEAD, HEAD).astype(F32) * scale
     return grown, gattn, in_sum, out_sum
 
 

time: 125 us -> 110 us (0.88)
  Pallas kernels: 113 us -> 100 us
  local copies, waits for them, and re-layouts: 9.39 us -> 3.99 us
  other arithmetic: 1.67 us -> 5.1 us
    pallas_call x1, Pallas kernels: 113 us -> 100 us  [local(): pl.pallas_call(functools.partial(kernel, (zs, dps, depth_k, k_in, k_out,...]
    unnamed x16 -> x4, local copies, waits for them, and re-layouts: 9.21 us -> 2.22 us
    mul x0 -> x3, other arithmetic: none -> 4.17 us  [the longest x1 3.01 us: local(): out_sum[:rows_o].reshape(rows_out, k_out, HEAD, HEAD).astype(F32) * scale]
    another operation x0 -> x2, local copies, waits for them, and re-layouts: none -> 1.52 us  [index_table(): flat, order = (jnp.stack(flats), jnp.stack(orders))]
    reduce_max x2 -> x1, other arithmetic: 1.5 us -> 0.1 us  [index_table(): found = jnp.max(jnp.where(same, order[:, None, :], -1), axis=2)]
where the time goes in v3:
time: 110 us
  Pallas kernels  100 us (91%)
  other arithmetic  5.1 us (5%)
  local copies, waits for them, and re-layouts  3.99 us (4%)
    pallas_call x1, Pallas kernels, local(): pl.pallas_call(functools.partial(kernel, (zs, dps, depth_k, k_in, k_out,...  100 us
    mul x1, other arithmetic, local(): out_sum[:rows_o].reshape(rows_out, k_out, HEAD, HEAD).astype(F32) * scale  3.01 us
    unnamed x4, local copies, waits for them, and re-layouts  2.22 us

profile of v3, /device:TPU:9, one launch (start us, length us, event | category | flops | bytes accessed | tf_op | source)
XLA Modules:
  0.0 109.9 jit_solution(2162642339149152423)
XLA Ops:
  0.6 0.8 stack.14
  1.4 0.8 stack.15
  2.2 0.1 add.43
  2.3 0.1 pad_add_fusion.1
  2.4 0.1 select_reduce_fusion
  2.5 0.1 reduce_max.12
  2.5 0.1 reshape.65
  2.6 0.7 pad_add_fusion.3.table
  3.4 0.0 copy-start
  3.4 0.7 copy-done
  4.0 100.1 %shard_map.120 = (bf16[128,2560]{1,0:T(8,128)(2,1)S(1)}, bf16[128,1280]{1,0:T(8,128)(2,1)S(1)}, bf16[5120,128]{1,0:T(8,128)(2,1)}, bf16[2560,128]{1,0:T(8,128)(2,1)S(1)}) custom-call(s32[226]{0:T(256)S(1)} %pad_add_fusion.3.table, f32[2]{0:T(128)S(1)} %copy-done, bf16[128,2560]{1,0:T(8,128)(2,1)} %attn_hbm.1, bf16[128,2560]{1,0:T(8,128)(2,1)} %cot_hbm.1, ...), custom_call_target="tpu_custom_call" | custom-call | tf_op jit(solution)/shard_map/pallas_call | solution.py:720
  104.1 3.0 %convert_multiply_fusion = f32[5120,128]{1,0:T(8,128)} fusion(bf16[5120,128]{1,0:T(8,128)(2,1)} %get-tuple-element.11), kind=kLoop, calls=%fused_computation | loop fusion | flops 1310720 | bytes 3932160 | tf_op jit(solution)/shard_map/mul | solution.py:770
  107.1 1.2 %convert_multiply_fusion.1 = f32[2560,128]{1,0:T(8,128)} fusion(bf16[2560,128]{1,0:T(8,128)(2,1)S(1)} %get-tuple-element.10), kind=kLoop, calls=%fused_computation.1 | loop fusion | flops 655360 | bytes 1966080 | tf_op jit(solution)/shard_map/mul | solution.py:769
  108.3 0.8 copy.15
  109.1 0.7 copy.16
  (6 shorter events, 0.0 us)
Async XLA Ops:
  3.4 0.7 copy-start

commit v4 on v3

--- a/solution.py
+++ b/solution.py
@@ -244,6 +244,26 @@
 
     lax.fori_loop(0, zs, og_start, 0)
 
+    def relay(s, q):
+        for way in range(2):
+            zz = z - s + 2 * s * way
+            nxt = z + 1 - 2 * way
+            f = 2 * zz + core
+
+            @pl.when((zz >= 0) & (zz < zs))
+            def _():
+                w_copy(f, h, q, way, other_dp).wait_recv()
+
+                @pl.when((nxt >= 0) & (nxt < zs))
+                def _():
+                    w_copy(f, h, q, way, above if way == 0 else below).start()
+
+                w_copy(f, h, q, 2, other_dp).start()
+                w_copy(f, h, q, 3, other_core).start()
+
+    for q in range(n_sub // 2):
+        relay(1, q)
+
     others[2].wait()
     others[3].wait()
 
@@ -257,6 +277,9 @@
     lax.fori_loop(0, rows_all, hid_row, 0, unroll=4)
     for b in range(nl):
         hid[:, b * HEAD : (b + 1) * HEAD] = sums[in_link(pairs + tn * nl + b)].astype(BF16)
+
+    for q in range(n_sub // 2, n_sub):
+        relay(1, q)
 
     hg_acc[...] = jnp.zeros_like(hg_acc)
 
@@ -272,7 +295,7 @@
             (og_mine[f * nb + b].astype(F32) + og_theirs[f * nb + b].astype(F32)).astype(BF16)
             for b in range(nb)
         ]
-        hg_acc[...] += dot(jnp.concatenate(blocks, axis=1), w_all[f], 1, 1)
+        hg_acc[...] += dot(w_all[f], jnp.concatenate(blocks, axis=1), 1, 1)
 
     def first(f, flip):
         @pl.when(flip == 1)
@@ -286,23 +309,6 @@
 
         forward(f)
 
-    def relay(s, q):
-        for way in range(2):
-            zz = z - s + 2 * s * way
-            nxt = z + 1 - 2 * way
-            f = 2 * zz + core
-
-            @pl.when((zz >= 0) & (zz < zs))
-            def _():
-                w_copy(f, h, q, way, other_dp).wait_recv()
-
-                @pl.when((nxt >= 0) & (nxt < zs))
-                def _():
-                    w_copy(f, h, q, way, above if way == 0 else below).start()
-
-                w_copy(f, h, q, 2, other_dp).start()
-                w_copy(f, h, q, 3, other_core).start()
-
     def pass_on(s, q):
         for way in range(2):
             zz = z - s + 2 * s * way
@@ -315,7 +321,10 @@
 
     def step(s, _):
         def part(q, _):
-            relay(s, q)
+            @pl.when(s >= 2)
+            def _():
+                relay(s, q)
+
             pass_on(s - (q == 0).astype(jnp.int32), (q + n_sub - 1) % n_sub)
             shard_of(s - 1, q, first)
 
@@ -336,7 +345,7 @@
     over_shards(zs - 1, backward)
 
     for b in range(nl):
-        hg_all[tn * nl + b] = hg_acc[:, b * HEAD : (b + 1) * HEAD].astype(BF16)
+        hg_all[tn * nl + b] = hg_acc[b * HEAD : (b + 1) * HEAD, :].T.astype(BF16)
     hg_copy(tn).start()
 
     def piece_copy(src, dst, send, recv, to):
@@ -428,8 +437,17 @@
 
             self.each_e(lambda e: self.each_q(lambda q: one(e, q)), True)
 
-        def dp_sums(self):
+        def dp_sums(self, rows_between, row):
+            each = -(-rows_between // zs)
+
             def one(q):
+                for i in range(each):
+                    r = q * each + i
+
+                    @pl.when(r < rows_between)
+                    def _():
+                        row(r)
+
                 rows = self.rows(core, dp, q)
                 total = self.g[rows, :].astype(F32)
                 for i in range(1, dps):
@@ -550,31 +568,25 @@
     outs.core_sums()
     ins.core_sums()
 
-    def grown_row(r, _):
+    def grown_row(r):
         cols = pl.ds(pl.multiple_of(r * HEAD, HEAD), HEAD)
         total = None
         for k in range(k_out):
-            j = r * k_out + k
-            term = dot(oo[out_col(r, k)], out_b[j])
+            term = dot(oo[out_col(r, k)], out_b[r * k_out + k])
             total = term if total is None else total + term
         grown[:, cols] = total.astype(BF16)
-        return 0
-
-    lax.fori_loop(0, rows_out, grown_row, 0, unroll=4)
-    outs.dp_sums()
-
-    def gattn_row(r, _):
+
+    def gattn_row(r):
         cols = pl.ds(pl.multiple_of(r * HEAD, HEAD), HEAD)
+        mine = tn * rows_in + r
         total = None
         for k in range(k_in):
-            j = (tn * rows_in + r) * k_in + k
-            term = dot(hg_all[in_col(tn * rows_in + r, k)], in_b[j], 1, 1)
+            term = dot(hg_all[in_col(mine, k)], in_b[mine * k_in + k], 1, 1)
             total = term if total is None else total + term
         gattn[:, cols] = total.astype(BF16)
-        return 0
-
-    lax.fori_loop(0, rows_in, gattn_row, 0, unroll=2)
-    ins.dp_sums()
+
+    outs.dp_sums(rows_out, grown_row)
+    ins.dp_sums(rows_in, gattn_row)
     outs.z_sums()
     ins.z_sums()
     outs.forward_z()
@@ -630,6 +642,35 @@
         return 0
 
     lax.fori_loop(0, (zs - 1) * n_sub, relay_done, 0)
+
+
+def finish_kernel(
+    scale, grown_in, gattn_in, out_in, in_in, grown, gattn, out_sum, in_sum, out_buf, in_buf, sems
+):
+    copies = [
+        pltpu.make_async_copy(grown_in, grown, sems.at[0]),
+        pltpu.make_async_copy(gattn_in, gattn, sems.at[1]),
+    ]
+    for one in copies:
+        one.start()
+    spot = 2
+    for src, buf, dst, parts in ((out_in, out_buf, out_sum, 4), (in_in, in_buf, in_sum, 2)):
+        blocks = buf.shape[0]
+        for i in range(parts):
+            lo, hi = blocks * i // parts, blocks * (i + 1) // parts
+
+            def block(b, _):
+                rows = pl.ds(pl.multiple_of(b * HEAD, HEAD), HEAD)
+                buf[b] = src[rows, :].astype(F32) * scale
+                return 0
+
+            lax.fori_loop(lo, hi, block, 0)
+            part = pl.ds(lo, hi - lo)
+            copies.append(pltpu.make_async_copy(buf.at[part], dst.at[part], sems.at[spot]))
+            copies[-1].start()
+            spot += 1
+    for one in copies:
+        one.wait()
 
 
 def index_table(pick, in_cols, out_cols, targets):
@@ -745,7 +786,7 @@
             pltpu.VMEM(blocks, BF16),
             pltpu.VMEM(blocks, BF16),
             pltpu.VMEM((tok, feats), BF16),
-            pltpu.VMEM((tok, feats), F32),
+            pltpu.VMEM((feats, tok), F32),
             pltpu.VMEM((n_in, tok, HEAD), BF16),
             dma((fsdp, 2, n_sub, 4)),
             dma((fsdp, 2, n_sub)),
@@ -766,8 +807,28 @@
         depth_coef,
         *arrays,
     )
-    in_sum = in_sum[:rows_i].reshape(rows_in, k_in, HEAD, HEAD).astype(F32) * scale
-    out_sum = out_sum[:rows_o].reshape(rows_out, k_out, HEAD, HEAD).astype(F32) * scale
+    anywhere = pl.BlockSpec(memory_space=pl.ANY)
+    out_blocks_shape = (pairs_out, HEAD, HEAD)
+    in_blocks_shape = (rows_in * k_in, HEAD, HEAD)
+    grown, gattn, out_sum, in_sum = pl.pallas_call(
+        functools.partial(finish_kernel, scale),
+        out_shape=(
+            jax.ShapeDtypeStruct(grown.shape, BF16),
+            jax.ShapeDtypeStruct(gattn.shape, BF16),
+            jax.ShapeDtypeStruct(out_blocks_shape, F32),
+            jax.ShapeDtypeStruct(in_blocks_shape, F32),
+        ),
+        in_specs=[anywhere, anywhere, vmem, vmem],
+        out_specs=(anywhere,) * 4,
+        scratch_shapes=[
+            pltpu.VMEM(out_blocks_shape, F32),
+            pltpu.VMEM(in_blocks_shape, F32),
+            dma((8,)),
+        ],
+        compiler_params=pltpu.CompilerParams(vmem_limit_bytes=16 * 2**20),
+    )(grown, gattn, out_sum, in_sum)
+    in_sum = in_sum.reshape(rows_in, k_in, HEAD, HEAD)
+    out_sum = out_sum.reshape(rows_out, k_out, HEAD, HEAD)
     return grown, gattn, in_sum, out_sum
 
 

time: 110 us -> 108 us (0.982)
  other arithmetic: 5.1 us -> 0.94 us
  Pallas kernels: 100 us -> 102 us
    mul x2 -> x0, other arithmetic: 4.16 us -> none  [the longest x1 3.01 us: local(): out_sum[:rows_o].reshape(rows_out, k_out, HEAD, HEAD).astype(F32) * scale]
    pallas_call x0 -> x1, Pallas kernels: none -> 2.3 us  [local(): pl.pallas_call(functools.partial(finish_kernel, scale), out_shape=(jax.Sh...]
where the time goes in v4:
time: 108 us; the launch traced here: 107 us
  Pallas kernels  102 us (94%)
  local copies, waits for them, and re-layouts  3.74 us (3%)
    pallas_call x1, Pallas kernels, local(): pl.pallas_call(functools.partial(kernel, (zs, dps, depth_k, k_in, k_out,...  99.7 us
    pallas_call x1, Pallas kernels, local(): pl.pallas_call(functools.partial(finish_kernel, scale), out_shape=(jax.Sh...  2.3 us

profile of v4, /device:TPU:9, one launch (start us, length us, event | category | flops | bytes accessed | tf_op | source)
XLA Modules:
  0.0 107.4 jit_solution(17145950226142614958)
XLA Ops:
  0.6 0.8 stack.14
  1.4 0.8 stack.15
  2.2 0.1 add.43
  2.2 0.1 pad_add_fusion.1
  2.3 0.1 reshape.63
  2.4 0.1 select_reduce_fusion
  2.5 0.1 reduce_max.12
  2.6 0.7 pad_add_fusion.3.table
  3.4 0.0 copy-start.1
  3.4 0.7 copy-done.1
  4.0 99.7 %shard_map.120 = (bf16[128,2560]{1,0:T(8,128)(2,1)S(1)}, bf16[128,1280]{1,0:T(8,128)(2,1)S(1)}, bf16[5120,128]{1,0:T(8,128)(2,1)}, bf16[2560,128]{1,0:T(8,128)(2,1)S(1)}) custom-call(s32[226]{0:T(256)S(1)} %pad_add_fusion.3.table, f32[2]{0:T(128)S(1)} %copy-done.1, bf16[128,2560]{1,0:T(8,128)(2,1)} %attn_hbm.1, bf16[128,2560]{1,0:T(8,128)(2,1)} %cot_hbm.1, ...), custom_call_target="tpu_custom_call" | custom-call | tf_op jit(solution)/shard_map/pallas_call | solution.py:761
  103.8 0.0 copy-start
  103.8 1.3 %copy-done = bf16[5120,128]{1,0:T(8,128)(2,1)S(1)} copy-done((bf16[5120,128]{1,0:T(8,128)(2,1)S(1)}, bf16[5120,128]{1,0:T(8,128)(2,1)}, u32[]{:S(2)}) %copy-start) | copy-done | bytes 1310744
  105.1 2.3 %shard_map.121 = (bf16[128,2560]{1,0:T(8,128)(2,1)}, bf16[128,1280]{1,0:T(8,128)(2,1)}, f32[40,128,128]{2,1,0:T(8,128)}, f32[20,128,128]{2,1,0:T(8,128)}) custom-call(bf16[128,2560]{1,0:T(8,128)(2,1)S(1)} %get-tuple-element.12.grown_in, bf16[128,1280]{1,0:T(8,128)(2,1)S(1)} %get-tuple-element.13.gattn_in, bf16[5120,128]{1,0:T(8,128)(2,1)S(1)} %copy-done, ...), custom_call_target="tpu_custom_call" | custom-call | tf_op jit(solution)/shard_map/pallas_call | solution.py:813
  (6 shorter events, 0.0 us)
Async XLA Ops:
  3.4 0.7 copy-start.1
  103.8 1.3 %copy-start = (bf16[5120,128]{1,0:T(8,128)(2,1)S(1)}, bf16[5120,128]{1,0:T(8,128)(2,1)}, u32[]{:S(2)}) copy-start(bf16[5120,128]{1,0:T(8,128)(2,1)} %get-tuple-element.14.out_in) | copy-start | bytes 3932164

commit v5 on v4

--- a/solution.py
+++ b/solution.py
@@ -542,30 +542,44 @@
 
     lax.fori_loop(0, 2 * zs, add_shard, 0)
 
-    def out_row(r, _):
+    def halves(stream, rows, terms, row):
+        half = stream.g.shape[0] // (2 * HEAD * terms)
+        whole = rows == 2 * half
+        unroll = max(n for n in (1, 2, 3, 4, 5) if half % n == 0) if whole else 1
+
+        def run(c):
+            def one(i, _):
+                r = c * half + i
+                if whole:
+                    row(r)
+                else:
+                    pl.when(r < rows)(lambda: row(r))
+                return 0
+
+            lax.fori_loop(0, half, one, 0, unroll=unroll)
+
+        run(1 - core)
+        stream.start_core()
+        run(core)
+
+    def out_row(r):
         cols = pl.ds(pl.multiple_of(r * HEAD, HEAD), HEAD)
         for k in range(k_out):
-            j = r * k_out + k
-            to = pl.ds(pl.multiple_of(j * HEAD, HEAD), HEAD)
+            to = pl.ds(pl.multiple_of((r * k_out + k) * HEAD, HEAD), HEAD)
             outs.g[to, :] = dot(oo[out_col(r, k)], cot[:, cols], 0, 0).astype(BF16)
-        return 0
-
-    lax.fori_loop(0, rows_out, out_row, 0, unroll=4)
-    outs.start_core()
-    hg_copy(1 - tn).wait_recv()
-
-    def in_row(r, _):
+
+    def in_row(r):
         mine = tn * rows_in + r
         mine_cols = pl.ds(pl.multiple_of(mine * HEAD, HEAD), HEAD)
         for k in range(k_in):
             block = hg_all[in_col(mine, k)]
             to = pl.ds(pl.multiple_of((r * k_in + k) * HEAD, HEAD), HEAD)
             ins.g[to, :] = dot(attn[:, mine_cols], block, 0, 0).astype(BF16)
-        return 0
-
-    lax.fori_loop(0, rows_in, in_row, 0, unroll=2)
-    ins.start_core()
+
+    halves(outs, rows_out, k_out, out_row)
     outs.core_sums()
+    hg_copy(1 - tn).wait_recv()
+    halves(ins, rows_in, k_in, in_row)
     ins.core_sums()
 
     def grown_row(r):

time: 108 us -> 107 us (level)
  no operation moved by 1% of the time
where the time goes in v5:
time: 107 us
  Pallas kernels  101 us (94%)
  local copies, waits for them, and re-layouts  3.74 us (3%)
    pallas_call x1, Pallas kernels, local(): pl.pallas_call(functools.partial(kernel, (zs, dps, depth_k, k_in, k_out,...  99.2 us
    pallas_call x1, Pallas kernels, local(): pl.pallas_call(functools.partial(finish_kernel, scale), out_shape=(jax.Sh...  2.3 us

profile of v5, /device:TPU:9, one launch (start us, length us, event | category | flops | bytes accessed | tf_op | source)
XLA Modules:
  0.0 106.8 jit_solution(17311841441437932666)
XLA Ops:
  0.6 0.8 stack.14
  1.4 0.8 stack.15
  2.2 0.1 add.43
  2.2 0.1 pad_add_fusion.1
  2.3 0.1 reshape.63
  2.4 0.1 select_reduce_fusion
  2.5 0.1 reduce_max.12
  2.6 0.7 pad_add_fusion.3.table
  3.4 0.0 copy-start.1
  3.4 0.7 copy-done.1
  4.0 99.2 %shard_map.120 = (bf16[128,2560]{1,0:T(8,128)(2,1)S(1)}, bf16[128,1280]{1,0:T(8,128)(2,1)S(1)}, bf16[5120,128]{1,0:T(8,128)(2,1)}, bf16[2560,128]{1,0:T(8,128)(2,1)S(1)}) custom-call(s32[226]{0:T(256)S(1)} %pad_add_fusion.3.table, f32[2]{0:T(128)S(1)} %copy-done.1, bf16[128,2560]{1,0:T(8,128)(2,1)} %attn_hbm.1, bf16[128,2560]{1,0:T(8,128)(2,1)} %cot_hbm.1, ...), custom_call_target="tpu_custom_call" | custom-call | tf_op jit(solution)/shard_map/pallas_call | solution.py:775
  103.2 0.0 copy-start
  103.2 1.3 %copy-done = bf16[5120,128]{1,0:T(8,128)(2,1)S(1)} copy-done((bf16[5120,128]{1,0:T(8,128)(2,1)S(1)}, bf16[5120,128]{1,0:T(8,128)(2,1)}, u32[]{:S(2)}) %copy-start) | copy-done | bytes 1310744
  104.5 2.3 %shard_map.121 = (bf16[128,2560]{1,0:T(8,128)(2,1)}, bf16[128,1280]{1,0:T(8,128)(2,1)}, f32[40,128,128]{2,1,0:T(8,128)}, f32[20,128,128]{2,1,0:T(8,128)}) custom-call(bf16[128,2560]{1,0:T(8,128)(2,1)S(1)} %get-tuple-element.12.grown_in, bf16[128,1280]{1,0:T(8,128)(2,1)S(1)} %get-tuple-element.13.gattn_in, bf16[5120,128]{1,0:T(8,128)(2,1)S(1)} %copy-done, ...), custom_call_target="tpu_custom_call" | custom-call | tf_op jit(solution)/shard_map/pallas_call | solution.py:827
  (6 shorter events, 0.0 us)
Async XLA Ops:
  3.4 0.7 copy-start.1
  103.2 1.3 %copy-start = (bf16[5120,128]{1,0:T(8,128)(2,1)S(1)}, bf16[5120,128]{1,0:T(8,128)(2,1)}, u32[]{:S(2)}) copy-start(bf16[5120,128]{1,0:T(8,128)(2,1)} %get-tuple-element.14.out_in) | copy-start | bytes 3932164
